TPU v7x, 512 devices: a whole 4x4x16 slice. The times are simulated.
512 devices in a mesh: dp: 16 (over x, z_hi, core), dap: 32 (over y, z_lo).
Axes of the slice: x: 4, y: 4, z: 16 (z_hi: 2, z_lo: 8; z = z_hi * 8 + z_lo), core: 2. Of those that a mesh axis runs over, the one named last changes fastest.
Arguments:
- pair_repr: bfloat16 [16, 128, 128, 128], P('dp', 'dap'), may hold values from -16 to 16
- pair_mask: int32 [16, 128, 128], P('dp', 'dap'), may hold values from 0 to 1, as said below
- cotangent: bfloat16 [16, 128, 128, 128], P('dp', 'dap'), may hold values from -6 to 6
- proj_weight: bfloat16 [2, 128, 640], replicated, may hold values from -0.5 to 0.5
- proj_bias: float32 [2, 640], replicated, may hold values from -3 to 3
- norm_gain: float32 [2, 256], replicated, may hold values from 0.1 to 1.9
- norm_shift: float32 [2, 256], replicated, may hold values from -3 to 3
- out_weight: bfloat16 [2, 128, 128], replicated, may hold values from -0.5 to 0.5
- out_bias: float32 [2, 128], replicated, may hold values from -3 to 3
Outputs:
- pair_grad: bfloat16 [16, 128, 128, 128], P('dp', 'dap')
- proj_weight_grad: float32 [2, 128, 640], replicated
- out_weight_grad: float32 [2, 128, 128], replicated
Inputs may be any that keep to these rules, and one draw needn't show every extreme that they name: pair_mask[c, i, j] is 1 exactly when residues i and j both lie below crop c's length, which is at least 64 and below 128.
All inputs are finite; a program needn't handle non-finite values.
Results may differ from a plain program's by a relative error of at most 0.015.
Values may be sent and summed in bfloat16 or wider, within the bound.
A program may use at most 64 MiB of HBM per device.

v0:
```python
import jax
import jax.numpy as jnp
from jax import lax
from jax.sharding import PartitionSpec as P

NORM_EPSILON = 1e-05


def layer_norm(values, gain_vec, shift_vec, norm_axis):
    mean_value = jnp.mean(values, axis=norm_axis, keepdims=True)
    centred = values - mean_value
    variance = jnp.mean(centred * centred, axis=norm_axis, keepdims=True)
    return centred * lax.rsqrt(variance + NORM_EPSILON) * gain_vec + shift_vec


def norm_pullback(values, gain_vec, shift_vec, norm_axis, upstream):
    _, pull_back = jax.vjp(
        lambda inner_value: layer_norm(inner_value, gain_vec, shift_vec, norm_axis), values
    )
    return pull_back(upstream)[0]


def edge_pair(edge_pre, cell_mask):
    left_edge = jax.nn.sigmoid(edge_pre[1]) * edge_pre[0] * cell_mask
    right_edge = jax.nn.sigmoid(edge_pre[3]) * edge_pre[2] * cell_mask
    return jnp.stack([left_edge, right_edge]).astype(jnp.bfloat16)


def edge_pullback(edge_pre, cell_mask, grad_pair):
    sig_left = jax.nn.sigmoid(edge_pre[1])
    sig_right = jax.nn.sigmoid(edge_pre[3])
    grad_left = grad_pair[0].astype(jnp.float32) * cell_mask
    grad_right = grad_pair[1].astype(jnp.float32) * cell_mask
    return jnp.stack(
        [
            grad_left * sig_left,
            grad_left * edge_pre[0] * sig_left * (1.0 - sig_left),
            grad_right * sig_right,
            grad_right * edge_pre[2] * sig_right * (1.0 - sig_right),
        ]
    ).astype(jnp.bfloat16)


def triangle(pair_edges, outgoing):
    if outgoing:
        einsum_form = "cik,cjk->cij"
    else:
        einsum_form = "cki,ckj->cij"
    return jnp.einsum(
        einsum_form, pair_edges[0], pair_edges[1], preferred_element_type=jnp.float32
    ).astype(jnp.bfloat16)


def triangle_pullback(pair_edges, grad_product, outgoing):
    left_edge = pair_edges[0]
    right_edge = pair_edges[1]
    if outgoing:
        grad_left = jnp.einsum(
            "cij,cjk->cik", grad_product, right_edge, preferred_element_type=jnp.float32
        )
        grad_right = jnp.einsum(
            "cij,cik->cjk", grad_product, left_edge, preferred_element_type=jnp.float32
        )
    else:
        grad_left = jnp.einsum(
            "ckj,cij->cki", right_edge, grad_product, preferred_element_type=jnp.float32
        )
        grad_right = jnp.einsum(
            "cki,cij->ckj", left_edge, grad_product, preferred_element_type=jnp.float32
        )
    return jnp.stack([grad_left, grad_right]).astype(jnp.bfloat16)


def update_weights(proj_weight, proj_bias, norm_gain, norm_shift, update, channels, hidden):
    w_edge = proj_weight[update, :, : 4 * hidden].reshape(channels, 4, hidden)
    w_gate = proj_weight[update, :, 4 * hidden :]
    bias_edge = proj_bias[update, : 4 * hidden].reshape(4, hidden, 1, 1)
    bias_gate = proj_bias[update, 4 * hidden :]
    gain_in = norm_gain[update, :channels]
    shift_in = norm_shift[update, :channels]
    gain_out = norm_gain[update, channels:][:, None, None]
    shift_out = norm_shift[update, channels:][:, None, None]
    return (w_edge, w_gate, bias_edge, bias_gate, gain_in, shift_in, gain_out, shift_out)


def shards(
    pair_repr,
    pair_mask,
    cotangent,
    proj_weight,
    proj_bias,
    norm_gain,
    norm_shift,
    out_weight,
    out_bias,
):
    channels = pair_repr.shape[3]
    hidden = out_weight.shape[1]
    pair_state = pair_repr[0]
    cell_mask = pair_mask[0].astype(jnp.float32)
    records = []
    for update in range(2):
        w_edge, w_gate, bias_edge, bias_gate, gain_in, shift_in, gain_out, shift_out = (
            update_weights(proj_weight, proj_bias, norm_gain, norm_shift, update, channels, hidden)
        )
        state_f = pair_state.astype(jnp.float32)
        normed = layer_norm(state_f, gain_in, shift_in, -1).astype(jnp.bfloat16)
        edge_pre = (
            jnp.einsum("rnc,cgh->ghrn", normed, w_edge, preferred_element_type=jnp.float32)
            + bias_edge
        )
        gate_pre = (
            jnp.einsum("rnc,cd->rnd", normed, w_gate, preferred_element_type=jnp.float32)
            + bias_gate
        )
        pair_edges = edge_pair(edge_pre, cell_mask)
        spread = lax.all_to_all(pair_edges, "dap", split_axis=1, concat_axis=2, tiled=True)
        product = lax.all_to_all(
            triangle(spread, update == 0), "dap", split_axis=1, concat_axis=0, tiled=True
        )
        mixed_norm = layer_norm(product.astype(jnp.float32), gain_out, shift_out, 0).astype(
            jnp.bfloat16
        )
        branch = (
            jnp.einsum(
                "hrn,hd->rnd", mixed_norm, out_weight[update], preferred_element_type=jnp.float32
            )
            + out_bias[update]
        )
        records.append(
            (state_f, normed, edge_pre, gate_pre, pair_edges, spread, product, mixed_norm, branch)
        )
        pair_state = (state_f + jax.nn.sigmoid(gate_pre) * branch).astype(jnp.bfloat16)
    upstream = cotangent[0].astype(jnp.float32)
    proj_grads = []
    out_grads = []
    for update in (1, 0):
        state_f, normed, edge_pre, gate_pre, pair_edges, spread, product, mixed_norm, branch = (
            records[update]
        )
        w_edge, w_gate, bias_edge, bias_gate, gain_in, shift_in, gain_out, shift_out = (
            update_weights(proj_weight, proj_bias, norm_gain, norm_shift, update, channels, hidden)
        )
        gate_value = jax.nn.sigmoid(gate_pre)
        grad_branch = (upstream * gate_value).astype(jnp.bfloat16)
        grad_gate = (upstream * branch * gate_value * (1.0 - gate_value)).astype(jnp.bfloat16)
        out_grad = jnp.einsum(
            "hrn,rnd->hd", mixed_norm, grad_branch, preferred_element_type=jnp.float32
        )
        grad_mixed = jnp.einsum(
            "rnd,hd->hrn", grad_branch, out_weight[update], preferred_element_type=jnp.float32
        )
        grad_product = norm_pullback(
            product.astype(jnp.float32), gain_out, shift_out, 0, grad_mixed
        ).astype(jnp.bfloat16)
        column_edges, column_stack = (
            lax.all_to_all(pair_edges, "dap", split_axis=1, concat_axis=2, tiled=True),
            lax.all_to_all(grad_product[None], "dap", split_axis=1, concat_axis=2, tiled=True),
        )
        column_grad = column_stack[0]
        grad_pair = lax.all_to_all(
            triangle_pullback(column_edges, column_grad, update == 0),
            "dap",
            split_axis=2,
            concat_axis=1,
            tiled=True,
        )
        grad_edge = edge_pullback(edge_pre, cell_mask, grad_pair)
        edge_grad = jnp.einsum(
            "rnc,ghrn->cgh", normed, grad_edge, preferred_element_type=jnp.float32
        ).reshape(channels, 4 * hidden)
        gate_grad = jnp.einsum("rnc,rnd->cd", normed, grad_gate, preferred_element_type=jnp.float32)
        grad_normed = jnp.einsum(
            "ghrn,cgh->rnc", grad_edge, w_edge, preferred_element_type=jnp.float32
        )
        grad_normed = grad_normed + jnp.einsum(
            "rnd,cd->rnc", grad_gate, w_gate, preferred_element_type=jnp.float32
        )
        upstream = upstream + norm_pullback(state_f, gain_in, shift_in, -1, grad_normed)
        proj_part = jnp.concatenate([edge_grad, gate_grad], axis=1)
        proj_grads.append(proj_part)
        out_grads.append(out_grad)
    proj_total = jnp.stack(proj_grads[::-1])
    out_total = jnp.stack(out_grads[::-1])
    proj_total, out_total = lax.psum((proj_total, out_total), ("dp", "dap"))
    return (upstream.astype(jnp.bfloat16)[None], proj_total, out_total)


def solution(mesh):
    placed = (
        P("dp", "dap", None, None),
        P("dp", "dap", None),
        P("dp", "dap", None, None),
        P(),
        P(),
        P(),
        P(),
        P(),
        P(),
    )
    return jax.shard_map(
        shards,
        mesh=mesh,
        in_specs=placed,
        out_specs=(P("dp", "dap", None, None), P(), P()),
        check_vma=False,
    )
```

profile of v0, /device:TPU:1, one launch (start us, length us, event | category | flops | bytes accessed | tf_op | source)
XLA Modules:
  0.0 692.3 jit_solution(13768532183465301370)
XLA Ops:
  7.2 1.1 copy.105
  9.7 0.7 copy-done.79
  10.4 0.7 copy-done.75
  11.0 1.2 slice_reduce_fusion.1
  13.1 34.6 %all_to_all.118 = bf16[2,128,4,128]{3,0,2,1:T(2,128)(2,1)S(1)} all-to-all(bf16[2,128,4,128]{3,0,2,1:T(2,128)(2,1)S(1)} %copy.110), channel_id=1, replica_groups=mesh['dp'=16,'dap'=32] {'dap'}, dimensions={1} | all-to-all | bytes 524288 | tf_op jit(solution)/shard_map/all_to_all | solution.py:117
  48.6 0.8 copy.112
  49.4 5.4 all-to-all-start.1
  56.3 10.3 %all-to-all-done.1 = bf16[4,128,128]{2,0,1:T(4,128)(2,1)S(1)} async-done(((bf16[4,128,128]{2,0,1:T(4,128)(2,1)}), bf16[4,128,128]{2,0,1:T(4,128)(2,1)S(1)}, u32[]{:S(2)}, u32[]{:S(2)}) %all-to-all-start.1) | async-done | bytes 131104 | tf_op jit(solution)/shard_map/all_to_all | solution.py:118
  68.4 1.0 convert_reduce_fusion.1
  71.0 25.2 %all_to_all.119 = bf16[2,128,4,128]{3,0,2,1:T(2,128)(2,1)S(1)} all-to-all(bf16[2,128,4,128]{3,0,2,1:T(2,128)(2,1)S(1)} %copy.119), channel_id=1, replica_groups=mesh['dp'=16,'dap'=32] {'dap'}, dimensions={1} | all-to-all | bytes 524288 | tf_op jit(solution)/shard_map/all_to_all | solution.py:157
  97.1 0.7 copy.125
  97.8 5.3 all-to-all-start.3
  104.0 1.1 fusion.15
  105.0 9.9 %all-to-all-done.3 = bf16[4,128,128]{2,0,1:T(4,128)(2,1)S(1)} async-done(((bf16[4,128,128]{2,0,1:T(4,128)(2,1)}), bf16[4,128,128]{2,0,1:T(4,128)(2,1)S(1)}, u32[]{:S(2)}, u32[]{:S(2)}) %all-to-all-start.3) | async-done | bytes 131104 | tf_op jit(solution)/shard_map/all_to_all | solution.py:118
  115.2 0.7 copy-done.17
  116.9 18.2 %all_to_all.120 = bf16[1,128,4,128]{3,2,0,1:T(4,128)(2,1)S(1)} all-to-all(bf16[1,128,4,128]{3,2,0,1:T(4,128)(2,1)S(1)} %copy.127), channel_id=1, replica_groups=mesh['dp'=16,'dap'=32] {'dap'}, dimensions={1} | all-to-all | bytes 262144 | tf_op jit(solution)/shard_map/all_to_all | solution.py:158
  135.2 0.9 copy-done.7
  136.3 0.7 copy-done.5
  137.2 0.9 copy.129
  138.1 6.7 all-to-all-start.5
  144.8 0.6 copy-done.78
  145.4 0.7 add.261
  146.1 0.7 copy-done.77
  146.8 0.7 mul.508
  147.6 0.7 copy-done.30
  148.4 0.7 copy-done.18
  149.4 14.0 %all-to-all-done.5 = bf16[2,4,128,128]{3,1,0,2:T(4,128)(2,1)} async-done(((bf16[2,4,128,128]{3,1,0,2:T(4,128)(2,1)}), bf16[2,4,128,128]{3,1,0,2:T(4,128)(2,1)}, u32[]{:S(2)}, u32[]{:S(2)}) %all-to-all-start.5) | async-done | bytes 262176 | tf_op jit(solution)/shard_map/all_to_all | solution.py:161
  163.4 1.0 copy.215
  164.5 0.7 copy-done.45
  166.7 1.0 fusion.36
  168.8 0.7 copy-done.19
  170.5 16.7 %all_to_all.121 = bf16[1,128,4,128]{3,2,0,1:T(4,128)(2,1)S(1)} all-to-all(bf16[1,128,4,128]{3,2,0,1:T(4,128)(2,1)S(1)} %copy.137), channel_id=1, replica_groups=mesh['dp'=16,'dap'=32] {'dap'}, dimensions={1} | all-to-all | bytes 262144 | tf_op jit(solution)/shard_map/all_to_all | solution.py:158
  187.2 0.9 copy-done.3
  188.2 0.7 copy-done.1
  189.2 0.9 copy.140
  190.1 6.1 all-to-all-start.7
  197.8 0.7 copy-done.21
  199.0 0.6 copy-done.40
  199.9 0.6 pad_maximum_fusion.7
  201.5 12.7 %all-to-all-done.7 = bf16[2,4,128,128]{3,1,0,2:T(4,128)(2,1)S(1)} async-done(((bf16[2,4,128,128]{3,1,0,2:T(4,128)(2,1)}), bf16[2,4,128,128]{3,1,0,2:T(4,128)(2,1)S(1)}, u32[]{:S(2)}, u32[]{:S(2)}) %all-to-all-start.7) | async-done | bytes 262176 | tf_op jit(solution)/shard_map/all_to_all | solution.py:161
  214.4 0.7 copy-done.46
  215.4 0.8 copy-done.11
  216.8 1.0 fusion.38
  217.8 0.9 pad_maximum_fusion
  219.7 0.8 copy.154
  220.5 462.3 %all-reduce.3.cloned.1.call-done = (f32[2,128,640]{2,1,0:T(8,128)}, f32[2,128,128]{2,1,0:T(8,128)}) async-done(((f32[2,128,640]{2,1,0:T(8,128)}, f32[2,128,128]{2,1,0:T(8,128)}), (f32[2,128,640]{2,1,0:T(8,128)}, f32[2,128,128]{2,1,0:T(8,128)})) %all-reduce.3.cloned.1.call-update) | async-done | bytes 786448 | tf_op jit(solution)/shard_map/psum | solution.py:185
  682.7 2.0 copy.220
  684.7 0.7 copy.221
  (242 shorter events, 20.7 us)
Async XLA Ops:
  7.2 1.8 copy-start.14
  8.9 59.5 %copy-start.32 = (f32[4,128]{1,0:T(4,128)}, f32[4,128]{1,0:T(4,128)S(1)}, u32[]{:S(2)}) copy-start(f32[4,128]{1,0:T(4,128)S(1)} %fusion.119) | copy-start | bytes 6148
  9.7 3.0 copy-start.10
  10.3 0.7 copy-start.76
  11.0 59.5 %copy-start.44 = (f32[4,128]{1,0:T(4,128)}, f32[4,128]{1,0:T(4,128)S(1)}, u32[]{:S(2)}) copy-start(f32[4,128]{1,0:T(4,128)S(1)} %convert_bitcast_fusion.1) | copy-start | bytes 6148
  12.2 56.2 %copy-start.57 = (f32[128]{0:T(128)}, f32[128]{0:T(128)S(1)}, u32[]{:S(2)}) copy-start(f32[128]{0:T(128)S(1)} %get-tuple-element.63) | copy-start | bytes 1540
  12.2 56.2 %copy-start.62 = (f32[128]{0:T(128)}, f32[128]{0:T(128)S(1)}, u32[]{:S(2)}) copy-start(f32[128]{0:T(128)S(1)} %get-tuple-element.78) | copy-start | bytes 1540
  12.2 57.9 %copy-start.66 = (f32[128]{0:T(128)}, f32[128]{0:T(128)S(1)}, u32[]{:S(2)}) copy-start(f32[128]{0:T(128)S(1)} %get-tuple-element.62) | copy-start | bytes 1540
  12.2 57.9 %copy-start.71 = (f32[128]{0:T(128)}, f32[128]{0:T(128)S(1)}, u32[]{:S(2)}) copy-start(f32[128]{0:T(128)S(1)} %get-tuple-element.75) | copy-start | bytes 1540
  49.4 17.2 %all-to-all-start.1 = ((bf16[4,128,128]{2,0,1:T(4,128)(2,1)}), bf16[4,128,128]{2,0,1:T(4,128)(2,1)S(1)}, u32[]{:S(2)}, u32[]{:S(2)}) async-start(bf16[4,128,128]{2,0,1:T(4,128)(2,1)} %copy.112), calls=%async_computation.1 | async-start | bytes 262144 | tf_op jit(solution)/shard_map/all_to_all | solution.py:118
  55.1 15.1 %copy-start.12 = (bf16[1,128,512]{1,2,0:T(8,128)(2,1)}, bf16[1,128,512]{1,2,0:T(8,128)(2,1)S(1)}, u32[]{:S(2)}) copy-start(bf16[1,128,512]{1,2,0:T(8,128)(2,1)S(1)} %copy.200) | copy-start | bytes 393220
  67.3 0.8 copy-start.16
  68.4 1.1 copy-start.8
  69.5 33.8 %copy-start.34 = (f32[4,128]{1,0:T(4,128)}, f32[4,128]{1,0:T(4,128)S(1)}, u32[]{:S(2)}) copy-start(f32[4,128]{1,0:T(4,128)S(1)} %fusion.121) | copy-start | bytes 6148
  97.8 5.3 copy-start.28
  97.8 17.1 %all-to-all-start.3 = ((bf16[4,128,128]{2,0,1:T(4,128)(2,1)}), bf16[4,128,128]{2,0,1:T(4,128)(2,1)S(1)}, u32[]{:S(2)}, u32[]{:S(2)}) async-start(bf16[4,128,128]{2,0,1:T(4,128)(2,1)} %copy.125), calls=%async_computation.3 | async-start | bytes 262144 | tf_op jit(solution)/shard_map/all_to_all | solution.py:118
  115.1 0.8 copy-start.17
  115.2 0.7 copy-start.60
  135.1 0.9 copy-start.7
  136.0 0.9 copy-start.5
  138.1 25.3 %all-to-all-start.5 = ((bf16[2,4,128,128]{3,1,0,2:T(4,128)(2,1)}), bf16[2,4,128,128]{3,1,0,2:T(4,128)(2,1)}, u32[]{:S(2)}, u32[]{:S(2)}) async-start(bf16[2,4,128,128]{3,1,0,2:T(4,128)(2,1)} %copy.129), calls=%async_computation.5 | async-start | bytes 524288 | tf_op jit(solution)/shard_map/all_to_all | solution.py:161
  147.5 0.7 copy-start.30
  147.5 0.7 copy-start.31
  147.5 0.7 copy-start.42
  148.3 0.8 copy-start.18
  165.2 0.9 copy-start.13
  165.5 0.9 copy-start.20
  165.5 0.9 copy-start.22
  165.5 0.9 copy-start.24
  165.5 0.9 copy-start.26
  166.7 1.0 copy-start.56
  166.7 1.0 copy-start.35
  166.7 1.6 copy-start.15
  167.7 1.0 copy-start.9
  167.8 1.0 copy-start.49
  168.7 0.8 copy-start.19
  187.1 0.9 copy-start.3
  188.0 0.9 copy-start.1
  190.1 6.1 copy-start.43
  190.1 24.0 %all-to-all-start.7 = ((bf16[2,4,128,128]{3,1,0,2:T(4,128)(2,1)}), bf16[2,4,128,128]{3,1,0,2:T(4,128)(2,1)S(1)}, u32[]{:S(2)}, u32[]{:S(2)}) async-start(bf16[2,4,128,128]{3,1,0,2:T(4,128)(2,1)} %copy.140), calls=%async_computation.7 | async-start | bytes 524288 | tf_op jit(solution)/shard_map/all_to_all | solution.py:161
  196.2 486.5 %all-reduce.3.cloned.1.call-start = ((), (), s32[]{:S(2)}) async-start(), calls=%async_computation.8 | async-start | bytes 1572864 | tf_op jit(solution)/shard_map/psum | solution.py:185
  196.9 0.9 copy-start.27
  197.6 0.9 copy-start.21
  197.6 1.0 copy-start.23
  197.6 1.0 copy-start.25
  215.3 0.9 copy-start.11
  216.8 1.0 copy-start.52
  682.7 2.0 copy-start.29
  (40 other events, 26.2 us)
Sparse Core Ops, SparseCore 0:
  218.9 463.8 all-reduce.2
where the time goes:
time: 694 us; the launch traced here: 692 us
  waiting for transfers between devices  509 us (73%)
  blocking collectives  94.8 us (14%)
  local copies, waits for them, and re-layouts  36.5 us (5%)
  starting transfers between devices  23.5 us (3%)
  between operations  15.1 us (2%)
  matrix products  8.93 us (1%)
    psum x1, waiting for transfers between devices, shards(): proj_total, out_total = lax.psum((proj_total, out_total), ('dp', 'dap'))  462 us
    all_to_all x2, blocking collectives, shards(): lax.all_to_all(pair_edges, 'dap', split_axis=1, concat_axis=2, tiled=True)  59.9 us
    all_to_all x2, blocking collectives, shards(): lax.all_to_all(grad_product[None], 'dap', split_axis=1, concat_axis=2, ti...  34.9 us
    all_to_all x2, waiting for transfers between devices, shards(): lax.all_to_all(triangle_pullback(column_edges, column_grad, update == 0),...  26.7 us
    unnamed x172, local copies, waits for them, and re-layouts  26.7 us
    all_to_all x2, waiting for transfers between devices, shards(): lax.all_to_all(triangle(spread, update == 0), 'dap', split_axis=1, concat...  20.2 us
  transfers between devices with their start and end apart: 5, of which 5 were waited for; matrix products, arithmetic and copies ran while one was open for 1% of the time, Pallas kernels for 0%

commit v1 on v0

--- a/solution.py
+++ b/solution.py
@@ -1,9 +1,105 @@
 import jax
 import jax.numpy as jnp
 from jax import lax
+from jax.experimental import pallas as pl
+from jax.experimental.pallas import tpu as pltpu
 from jax.sharding import PartitionSpec as P
 
 NORM_EPSILON = 1e-05
+MESH = pl.DeviceIdType.MESH
+
+
+def reduce_kernel(part_ref, total_ref, plane_buf, z_send, z_buf, own_total, all_buf, sems):
+    dp = lax.axis_index("dp")
+    dap = lax.axis_index("dap")
+    core, z_hi, x = dp % 2, (dp // 2) % 2, dp // 4
+    y, z_lo = dap // 8, dap % 8
+    member = (x * 4 + y) * 2 + core
+    z = z_hi * 8 + z_lo
+
+    def plane_device(j):
+        return ((j // 8) * 4 + z_hi * 2 + j % 2, ((j // 2) % 4) * 8 + z_lo)
+
+    def line_device(k):
+        return (x * 4 + (k // 8) * 2 + core, y * 8 + k % 8)
+
+    barrier = pltpu.get_barrier_semaphore()
+
+    @pl.loop(1, 32)
+    def _(k):
+        pl.semaphore_signal(
+            barrier, inc=1, device_id=plane_device((member + k) % 32), device_id_type=MESH
+        )
+
+    @pl.loop(1, 16)
+    def _(k):
+        pl.semaphore_signal(
+            barrier, inc=1, device_id=line_device((z + k) % 16), device_id_type=MESH
+        )
+
+    pl.semaphore_wait(barrier, 46)
+
+    def remote(source, target, step, device):
+        return pltpu.make_async_remote_copy(
+            src_ref=source,
+            dst_ref=target,
+            send_sem=sems.at[2 * step],
+            recv_sem=sems.at[2 * step + 1],
+            device_id=device,
+            device_id_type=MESH,
+        )
+
+    @pl.loop(1, 32)
+    def _(k):
+        j = (member + k) % 32
+        remote(part_ref.at[j], plane_buf.at[member], 0, plane_device(j)).start()
+
+    pltpu.make_async_copy(part_ref.at[member], plane_buf.at[member], sems.at[1]).start()
+    pltpu.make_async_copy(plane_buf, plane_buf, sems.at[1]).wait()
+    z_send[...] = jnp.sum(plane_buf[...].astype(jnp.float32), axis=0).astype(jnp.bfloat16)
+
+    @pl.loop(1, 16)
+    def _(k):
+        remote(z_send, z_buf.at[z], 1, line_device((z + k) % 16)).start()
+
+    pltpu.make_async_copy(z_send, z_buf.at[z], sems.at[3]).start()
+    pltpu.make_async_copy(z_buf, z_buf, sems.at[3]).wait()
+    own_total[...] = jnp.sum(z_buf[...].astype(jnp.float32), axis=0).astype(jnp.bfloat16)
+
+    @pl.loop(1, 32)
+    def _(k):
+        remote(own_total, all_buf.at[member], 2, plane_device((member + k) % 32)).start()
+
+    pltpu.make_async_copy(own_total, all_buf.at[member], sems.at[5]).start()
+    pltpu.make_async_copy(all_buf, all_buf, sems.at[5]).wait()
+    total_ref[...] = all_buf[...].astype(jnp.float32)
+    sent = plane_buf.at[pl.ds(0, 31)]
+    pltpu.make_async_copy(sent, sent, sems.at[0]).wait()
+    sent = z_buf.at[pl.ds(0, 15)]
+    pltpu.make_async_copy(sent, sent, sems.at[2]).wait()
+    sent = all_buf.at[pl.ds(0, 31)]
+    pltpu.make_async_copy(sent, sent, sems.at[4]).wait()
+
+
+def reduce_everywhere(part):
+    rows = part.shape[1]
+    return pl.pallas_call(
+        reduce_kernel,
+        out_shape=jax.ShapeDtypeStruct(part.shape, jnp.float32),
+        in_specs=[pl.BlockSpec(memory_space=pltpu.VMEM)],
+        out_specs=pl.BlockSpec(memory_space=pltpu.VMEM),
+        scratch_shapes=[
+            pltpu.VMEM((32, rows, 128), jnp.bfloat16),
+            pltpu.VMEM((rows, 128), jnp.bfloat16),
+            pltpu.VMEM((16, rows, 128), jnp.bfloat16),
+            pltpu.VMEM((rows, 128), jnp.bfloat16),
+            pltpu.VMEM((32, rows, 128), jnp.bfloat16),
+            pltpu.SemaphoreType.DMA((6,)),
+        ],
+        compiler_params=pltpu.CompilerParams(
+            collective_id=1, has_side_effects=True, vmem_limit_bytes=32 << 20
+        ),
+    )(part)
 
 
 def layer_norm(values, gain_vec, shift_vec, norm_axis):
@@ -182,7 +278,10 @@
         out_grads.append(out_grad)
     proj_total = jnp.stack(proj_grads[::-1])
     out_total = jnp.stack(out_grads[::-1])
-    proj_total, out_total = lax.psum((proj_total, out_total), ("dp", "dap"))
+    part = jnp.concatenate([proj_total.reshape(1280, 128), out_total.reshape(256, 128)])
+    total = reduce_everywhere(part.astype(jnp.bfloat16).reshape(32, 48, 128)).reshape(1536, 128)
+    proj_total = total[:1280].reshape(2, 128, 640)
+    out_total = total[1280:].reshape(2, 128, 128)
     return (upstream.astype(jnp.bfloat16)[None], proj_total, out_total)
 
 

time: 694 us -> 253 us (0.36)
  waiting for transfers between devices: 509 us -> 58.4 us
  Pallas kernels: 0 us -> 36.7 us
  blocking collectives: 94.8 us -> 78.1 us
  between operations: 15.1 us -> 1.78 us
    psum x1 -> x0, waiting for transfers between devices: 462 us -> none  [shards(): proj_total, out_total = lax.psum((proj_total, out_total), ('dp', 'dap'))]
    pallas_call x0 -> x1, Pallas kernels: none -> 36.7 us  [reduce_everywhere(): pl.pallas_call(reduce_kernel, out_shape=jax.ShapeDtypeStruct(part.shape,...]
    all_to_all x2 -> x1, blocking collectives: 34.9 us -> 18.2 us  [shards(): lax.all_to_all(grad_product[None], 'dap', split_axis=1, concat_axis=2, ti...]
    all_to_all x0 -> x1, waiting for transfers between devices: none -> 10.3 us  [shards(): lax.all_to_all(grad_product[None], 'dap', split_axis=1, concat_axis=2, ti...]
    unnamed x172 -> x168, local copies, waits for them, and re-layouts: 26.7 us -> 23 us
  transfers between devices with their start and end apart: 5 -> 5, of which waited for: 5 -> 5; matrix products, arithmetic and copies ran while one was open for 1% -> 3% of each run, Pallas kernels for 0% -> 0%
where the time goes in v1:
time: 253 us; the launch traced here: 252 us
  blocking collectives  78.1 us (31%)
  waiting for transfers between devices  58.4 us (23%)
  Pallas kernels  36.7 us (15%)
  local copies, waits for them, and re-layouts  35.5 us (14%)
  starting transfers between devices  28.9 us (11%)
  matrix products  9.62 us (4%)
  other arithmetic  2.68 us (1%)
    all_to_all x2, blocking collectives, shards(): lax.all_to_all(pair_edges, 'dap', split_axis=1, concat_axis=2, tiled=True)  59.9 us
    pallas_call x1, Pallas kernels, reduce_everywhere(): pl.pallas_call(reduce_kernel, out_shape=jax.ShapeDtypeStruct(part.shape,...  36.7 us
    all_to_all x2, waiting for transfers between devices, shards(): lax.all_to_all(triangle_pullback(column_edges, column_grad, update == 0),...  28 us
    unnamed x168, local copies, waits for them, and re-layouts  23 us
    all_to_all x2, waiting for transfers between devices, shards(): lax.all_to_all(triangle(spread, update == 0), 'dap', split_axis=1, concat...  20.1 us
    all_to_all x1, blocking collectives, shards(): lax.all_to_all(grad_product[None], 'dap', split_axis=1, concat_axis=2, ti...  18.2 us
    all_to_all x2, starting transfers between devices, shards(): lax.all_to_all(triangle_pullback(column_edges, column_grad, update == 0),...  13 us
    all_to_all x2, starting transfers between devices, shards(): lax.all_to_all(triangle(spread, update == 0), 'dap', split_axis=1, concat...  10.7 us
  transfers between devices with their start and end apart: 5, of which 5 were waited for; matrix products, arithmetic and copies ran while one was open for 3% of the time, Pallas kernels for 0%

profile of v1, /device:TPU:1, one launch (start us, length us, event | category | flops | bytes accessed | tf_op | source)
XLA Modules:
  0.0 251.7 jit_solution(18266399883026941818)
XLA Ops:
  0.6 1.1 copy.105
  3.1 0.7 copy-done.78
  3.8 0.7 copy-done.74
  4.5 1.1 slice_reduce_fusion.1
  6.5 34.6 %all_to_all.118 = bf16[2,128,4,128]{3,0,2,1:T(2,128)(2,1)S(1)} all-to-all(bf16[2,128,4,128]{3,0,2,1:T(2,128)(2,1)S(1)} %copy.110), channel_id=1, replica_groups=mesh['dp'=16,'dap'=32] {'dap'}, dimensions={1} | all-to-all | bytes 524288 | tf_op jit(solution)/shard_map/all_to_all | solution.py:213
  42.0 0.8 copy.112
  42.8 5.4 %all-to-all-start.1 = ((bf16[4,128,128]{2,0,1:T(4,128)(2,1)}), bf16[4,128,128]{2,0,1:T(4,128)(2,1)S(1)}, u32[]{:S(2)}, u32[]{:S(2)}) async-start(bf16[4,128,128]{2,0,1:T(4,128)(2,1)} %copy.112), calls=%async_computation.1 | async-start | bytes 262144 | tf_op jit(solution)/shard_map/all_to_all | solution.py:214
  49.7 10.3 %all-to-all-done.1 = bf16[4,128,128]{2,0,1:T(4,128)(2,1)S(1)} async-done(((bf16[4,128,128]{2,0,1:T(4,128)(2,1)}), bf16[4,128,128]{2,0,1:T(4,128)(2,1)S(1)}, u32[]{:S(2)}, u32[]{:S(2)}) %all-to-all-start.1) | async-done | bytes 131104 | tf_op jit(solution)/shard_map/all_to_all | solution.py:214
  61.3 1.0 convert_reduce_fusion.1
  63.9 25.3 %all_to_all.119 = bf16[2,128,4,128]{3,0,2,1:T(2,128)(2,1)S(1)} all-to-all(bf16[2,128,4,128]{3,0,2,1:T(2,128)(2,1)S(1)} %copy.119), channel_id=1, replica_groups=mesh['dp'=16,'dap'=32] {'dap'}, dimensions={1} | all-to-all | bytes 524288 | tf_op jit(solution)/shard_map/all_to_all | solution.py:253
  90.0 0.7 copy.125
  90.7 5.3 %all-to-all-start.3 = ((bf16[4,128,128]{2,0,1:T(4,128)(2,1)}), bf16[4,128,128]{2,0,1:T(4,128)(2,1)S(1)}, u32[]{:S(2)}, u32[]{:S(2)}) async-start(bf16[4,128,128]{2,0,1:T(4,128)(2,1)} %copy.125), calls=%async_computation.3 | async-start | bytes 262144 | tf_op jit(solution)/shard_map/all_to_all | solution.py:214
  96.2 0.6 copy-done.64
  96.9 1.1 fusion.15
  98.0 9.9 %all-to-all-done.3 = bf16[4,128,128]{2,0,1:T(4,128)(2,1)S(1)} async-done(((bf16[4,128,128]{2,0,1:T(4,128)(2,1)}), bf16[4,128,128]{2,0,1:T(4,128)(2,1)S(1)}, u32[]{:S(2)}, u32[]{:S(2)}) %all-to-all-start.3) | async-done | bytes 131104 | tf_op jit(solution)/shard_map/all_to_all | solution.py:214
  108.1 0.7 copy-done.17
  109.8 18.2 %all_to_all.120 = bf16[1,128,4,128]{3,2,0,1:T(4,128)(2,1)S(1)} all-to-all(bf16[1,128,4,128]{3,2,0,1:T(4,128)(2,1)S(1)} %copy.127), channel_id=1, replica_groups=mesh['dp'=16,'dap'=32] {'dap'}, dimensions={1} | all-to-all | bytes 262144 | tf_op jit(solution)/shard_map/all_to_all | solution.py:254
  128.1 0.9 copy-done.7
  129.1 0.7 copy-done.5
  130.0 0.9 copy.129
  130.9 6.7 %all-to-all-start.5 = ((bf16[2,4,128,128]{3,1,0,2:T(4,128)(2,1)}), bf16[2,4,128,128]{3,1,0,2:T(4,128)(2,1)}, u32[]{:S(2)}, u32[]{:S(2)}) async-start(bf16[2,4,128,128]{3,1,0,2:T(4,128)(2,1)} %copy.129), calls=%async_computation.5 | async-start | bytes 524288 | tf_op jit(solution)/shard_map/all_to_all | solution.py:257
  138.3 0.7 add.257
  139.6 0.7 mul.508
  140.3 0.7 copy-done.30
  141.2 0.7 copy-done.18
  142.1 14.1 %all-to-all-done.5 = bf16[2,4,128,128]{3,1,0,2:T(4,128)(2,1)} async-done(((bf16[2,4,128,128]{3,1,0,2:T(4,128)(2,1)}), bf16[2,4,128,128]{3,1,0,2:T(4,128)(2,1)}, u32[]{:S(2)}, u32[]{:S(2)}) %all-to-all-start.5) | async-done | bytes 262176 | tf_op jit(solution)/shard_map/all_to_all | solution.py:257
  156.3 1.0 copy.211
  157.4 0.7 copy-done.42
  159.7 1.0 fusion.44
  161.8 0.7 copy-done.19
  163.3 0.8 copy.137
  164.1 5.2 %all-to-all-start.6 = ((bf16[1,128,4,128]{3,2,0,1:T(4,128)(2,1)}), bf16[1,128,4,128]{3,2,0,1:T(4,128)(2,1)S(1)}, u32[]{:S(2)}, u32[]{:S(2)}) async-start(bf16[1,128,4,128]{3,2,0,1:T(4,128)(2,1)} %copy.137), calls=%async_computation.6 | async-start | bytes 262144 | tf_op jit(solution)/shard_map/all_to_all | solution.py:254
  170.0 0.8 fusion.28
  170.8 10.3 %all-to-all-done.6 = bf16[1,128,4,128]{3,2,0,1:T(4,128)(2,1)S(1)} async-done(((bf16[1,128,4,128]{3,2,0,1:T(4,128)(2,1)}), bf16[1,128,4,128]{3,2,0,1:T(4,128)(2,1)S(1)}, u32[]{:S(2)}, u32[]{:S(2)}) %all-to-all-start.6) | async-done | bytes 131104 | tf_op jit(solution)/shard_map/all_to_all | solution.py:254
  181.2 0.9 copy-done.3
  182.2 0.7 copy-done.1
  183.2 0.9 copy.140
  184.1 6.2 %all-to-all-start.7 = ((bf16[2,4,128,128]{3,1,0,2:T(4,128)(2,1)}), bf16[2,4,128,128]{3,1,0,2:T(4,128)(2,1)S(1)}, u32[]{:S(2)}, u32[]{:S(2)}) async-start(bf16[2,4,128,128]{3,1,0,2:T(4,128)(2,1)} %copy.140), calls=%async_computation.7 | async-start | bytes 524288 | tf_op jit(solution)/shard_map/all_to_all | solution.py:257
  190.7 0.6 copy-done.21
  193.4 0.6 copy-done.47
  194.3 13.9 %all-to-all-done.7 = bf16[2,4,128,128]{3,1,0,2:T(4,128)(2,1)S(1)} async-done(((bf16[2,4,128,128]{3,1,0,2:T(4,128)(2,1)}), bf16[2,4,128,128]{3,1,0,2:T(4,128)(2,1)S(1)}, u32[]{:S(2)}, u32[]{:S(2)}) %all-to-all-start.7) | async-done | bytes 262176 | tf_op jit(solution)/shard_map/all_to_all | solution.py:257
  208.4 0.7 copy-done.43
  210.0 36.7 %shard_map.112 = f32[32,48,128]{2,1,0:T(8,128)S(1)} custom-call(bf16[32,48,128]{2,1,0:T(8,128)(2,1)S(1)} %bitcast.315), custom_call_target="tpu_custom_call" | custom-call | tf_op jit(solution)/shard_map/pallas_call | solution.py:86
  246.8 0.7 slice.199
  248.0 1.0 reshape.255
  249.0 0.9 fusion.46
  250.1 0.6 copy-done.45
  250.9 0.8 copy.154
  (242 shorter events, 20.7 us)
Async XLA Ops:
  0.6 1.8 copy-start.14
  2.4 58.9 %copy-start.46 = (f32[4,128]{1,0:T(4,128)}, f32[4,128]{1,0:T(4,128)S(1)}, u32[]{:S(2)}) copy-start(f32[4,128]{1,0:T(4,128)S(1)} %fusion.127) | copy-start | bytes 6148
  3.1 2.9 %copy-start.10 = (bf16[1,128,512]{1,2,0:T(8,128)(2,1)}, bf16[1,128,512]{1,2,0:T(8,128)(2,1)S(1)}, u32[]{:S(2)}) copy-start(bf16[1,128,512]{1,2,0:T(8,128)(2,1)S(1)} %copy.108) | copy-start | bytes 393220
  4.5 58.9 %copy-start.41 = (f32[4,128]{1,0:T(4,128)}, f32[4,128]{1,0:T(4,128)S(1)}, u32[]{:S(2)}) copy-start(f32[4,128]{1,0:T(4,128)S(1)} %convert_bitcast_fusion.1) | copy-start | bytes 6148
  5.6 55.6 %copy-start.61 = (f32[128]{0:T(128)}, f32[128]{0:T(128)S(1)}, u32[]{:S(2)}) copy-start(f32[128]{0:T(128)S(1)} %get-tuple-element.61) | copy-start | bytes 1540
  5.6 55.6 %copy-start.67 = (f32[128]{0:T(128)}, f32[128]{0:T(128)S(1)}, u32[]{:S(2)}) copy-start(f32[128]{0:T(128)S(1)} %get-tuple-element.76) | copy-start | bytes 1540
  5.6 57.3 %copy-start.63 = (f32[128]{0:T(128)}, f32[128]{0:T(128)S(1)}, u32[]{:S(2)}) copy-start(f32[128]{0:T(128)S(1)} %get-tuple-element.60) | copy-start | bytes 1540
  5.7 57.3 %copy-start.70 = (f32[128]{0:T(128)}, f32[128]{0:T(128)S(1)}, u32[]{:S(2)}) copy-start(f32[128]{0:T(128)S(1)} %get-tuple-element.73) | copy-start | bytes 1540
  42.8 17.2 %all-to-all-start.1 = ((bf16[4,128,128]{2,0,1:T(4,128)(2,1)}), bf16[4,128,128]{2,0,1:T(4,128)(2,1)S(1)}, u32[]{:S(2)}, u32[]{:S(2)}) async-start(bf16[4,128,128]{2,0,1:T(4,128)(2,1)} %copy.112), calls=%async_computation.1 | async-start | bytes 262144 | tf_op jit(solution)/shard_map/all_to_all | solution.py:214
  48.5 14.5 %copy-start.12 = (bf16[1,128,512]{1,2,0:T(8,128)(2,1)}, bf16[1,128,512]{1,2,0:T(8,128)(2,1)S(1)}, u32[]{:S(2)}) copy-start(bf16[1,128,512]{1,2,0:T(8,128)(2,1)S(1)} %copy.199) | copy-start | bytes 393220
  60.2 0.8 copy-start.16
  61.3 1.1 copy-start.8
  62.4 33.8 %copy-start.32 = (f32[4,128]{1,0:T(4,128)}, f32[4,128]{1,0:T(4,128)S(1)}, u32[]{:S(2)}) copy-start(f32[4,128]{1,0:T(4,128)S(1)} %fusion.129) | copy-start | bytes 6148
  90.7 5.3 %copy-start.28 = (bf16[1,4,128,128]{3,2,1,0:T(8,128)(2,1)S(1)}, bf16[1,4,128,128]{3,2,1,0:T(8,128)(2,1)}, u32[]{:S(2)}) copy-start(bf16[1,4,128,128]{3,2,1,0:T(8,128)(2,1)} %param.11) | copy-start | bytes 393220
  90.7 17.1 %all-to-all-start.3 = ((bf16[4,128,128]{2,0,1:T(4,128)(2,1)}), bf16[4,128,128]{2,0,1:T(4,128)(2,1)S(1)}, u32[]{:S(2)}, u32[]{:S(2)}) async-start(bf16[4,128,128]{2,0,1:T(4,128)(2,1)} %copy.125), calls=%async_computation.3 | async-start | bytes 262144 | tf_op jit(solution)/shard_map/all_to_all | solution.py:214
  108.0 0.8 copy-start.17
  108.1 0.7 copy-start.57
  128.0 0.9 copy-start.7
  128.9 0.9 copy-start.5
  130.9 25.3 %all-to-all-start.5 = ((bf16[2,4,128,128]{3,1,0,2:T(4,128)(2,1)}), bf16[2,4,128,128]{3,1,0,2:T(4,128)(2,1)}, u32[]{:S(2)}, u32[]{:S(2)}) async-start(bf16[2,4,128,128]{3,1,0,2:T(4,128)(2,1)} %copy.129), calls=%async_computation.5 | async-start | bytes 524288 | tf_op jit(solution)/shard_map/all_to_all | solution.py:257
  140.3 0.7 copy-start.39
  141.0 0.8 copy-start.18
  158.1 0.9 copy-start.13
  158.4 0.9 copy-start.20
  158.4 0.9 copy-start.22
  158.4 0.9 copy-start.24
  158.4 0.9 copy-start.26
  159.7 1.0 copy-start.55
  159.7 1.0 copy-start.33
  159.7 1.6 copy-start.15
  160.7 1.0 copy-start.9
  160.8 1.0 copy-start.48
  161.6 0.8 copy-start.19
  164.1 5.3 %copy-start.40 = (f32[4,128]{1,0:T(4,128)S(1)}, f32[4,128]{1,0:T(4,128)}, u32[]{:S(2)}) copy-start(f32[4,128]{1,0:T(4,128)} %copy-done.38) | copy-start | bytes 6148
  164.1 17.0 %all-to-all-start.6 = ((bf16[1,128,4,128]{3,2,0,1:T(4,128)(2,1)}), bf16[1,128,4,128]{3,2,0,1:T(4,128)(2,1)S(1)}, u32[]{:S(2)}, u32[]{:S(2)}) async-start(bf16[1,128,4,128]{3,2,0,1:T(4,128)(2,1)} %copy.137), calls=%async_computation.6 | async-start | bytes 262144 | tf_op jit(solution)/shard_map/all_to_all | solution.py:254
  181.1 0.9 copy-start.3
  182.0 0.9 copy-start.1
  184.1 6.3 %copy-start.34 = (f32[4,128]{1,0:T(4,128)S(1)}, f32[4,128]{1,0:T(4,128)}, u32[]{:S(2)}) copy-start(f32[4,128]{1,0:T(4,128)} %copy-done.32) | copy-start | bytes 6148
  184.1 6.3 %copy-start.66 = (f32[128]{0:T(128)S(1)}, f32[128]{0:T(128)}, u32[]{:S(2)}) copy-start(f32[128]{0:T(128)} %copy-done.63) | copy-start | bytes 1540
  184.1 6.3 %copy-start.72 = (f32[128]{0:T(128)S(1)}, f32[128]{0:T(128)}, u32[]{:S(2)}) copy-start(f32[128]{0:T(128)} %copy-done.70) | copy-start | bytes 1540
  184.1 6.6 %copy-start.27 = (bf16[1,128,4,128]{3,1,0,2:T(8,128)(2,1)S(1)}, bf16[1,128,4,128]{3,1,0,2:T(8,128)(2,1)}, u32[]{:S(2)}) copy-start(bf16[1,128,4,128]{3,1,0,2:T(8,128)(2,1)} %copy-done.26) | copy-start | bytes 393220
  184.1 24.1 %all-to-all-start.7 = ((bf16[2,4,128,128]{3,1,0,2:T(4,128)(2,1)}), bf16[2,4,128,128]{3,1,0,2:T(4,128)(2,1)S(1)}, u32[]{:S(2)}, u32[]{:S(2)}) async-start(bf16[2,4,128,128]{3,1,0,2:T(4,128)(2,1)} %copy.140), calls=%async_computation.7 | async-start | bytes 524288 | tf_op jit(solution)/shard_map/all_to_all | solution.py:257
  190.4 0.9 copy-start.21
  190.4 1.0 copy-start.23
  190.4 1.0 copy-start.25
  192.6 0.8 copy-start.29
  246.8 1.0 copy-start.11
  249.0 1.0 copy-start.51
  (39 other events, 25.7 us)

commit v2 on v0

v2 whole, which is shorter than its diff:
```python
import jax
import jax.numpy as jnp
from jax import lax
from jax.experimental import pallas as pl
from jax.experimental.pallas import tpu as pltpu
from jax.sharding import PartitionSpec as P

NORM_EPSILON = 1e-05
MESH = pl.DeviceIdType.MESH
F32 = jnp.float32
BF16 = jnp.bfloat16
EDGES, PRODUCTS, D_PRODUCTS, D_EDGES = 0, 2, 4, 6
GAIN_IN, SHIFT_IN, GAIN_OUT, SHIFT_OUT, OUT_BIAS = 5, 6, 7, 8, 9
TO_OWNER, FROM_OWNER, BY_CHANNEL, BY_SOURCE = 0, 1, 2, 3


def dot(a, b):
    return jnp.dot(a, b, preferred_element_type=F32)


def dot_nt(a, b):
    return lax.dot_general(a, b, (((1,), (1,)), ((), ())), preferred_element_type=F32)


def transposed(a):
    return a.astype(F32).T.astype(BF16)


def sigmoid(a):
    return 0.5 * jnp.tanh(0.5 * a) + 0.5


def channel_mean(a):
    return jnp.sum(a, axis=0, keepdims=True) * (1.0 / a.shape[0])


def normalise(values):
    centred = values - channel_mean(values)
    scale = lax.rsqrt(channel_mean(centred * centred) + NORM_EPSILON)
    return centred * scale, scale


def norm_pullback(unit, scale, d_unit):
    return scale * (d_unit - channel_mean(d_unit) - unit * channel_mean(d_unit * unit))


def each(count, body):
    for step in range(count):
        body(step)


def kernel(
    pair_ref,
    mask_ref,
    cot_ref,
    w_ref,
    bias_ref,
    gain_ref,
    shift_ref,
    wo_ref,
    ob_ref,
    grad_ref,
    proj_ref,
    out_ref,
    w_t,
    wo_t,
    perm,
    col,
    state,
    normed,
    unit_in,
    scale_in,
    edge,
    gate,
    branch,
    unit_out,
    scale_out,
    mixed,
    up,
    d_edge,
    d_branch,
    cm,
    own,
    own_out,
    edge_send,
    edge_recv,
    prod_send,
    prod_recv,
    dprod_send,
    dprod_recv,
    dedge_send,
    dedge_recv,
    sum_send,
    plane_buf,
    z_send,
    z_buf,
    own_total,
    all_buf,
    sems,
):
    dp = lax.axis_index("dp")
    dap = lax.axis_index("dap")
    core, z_hi, x = dp % 2, (dp // 2) % 2, dp // 4
    y, z_lo = dap // 8, dap % 8
    member = (x * 4 + y) * 2 + core
    z = z_hi * 8 + z_lo

    def plane_device(j):
        return ((j // 8) * 4 + z_hi * 2 + j % 2, ((j // 2) % 4) * 8 + z_lo)

    def line_device(k):
        return (x * 4 + (k // 8) * 2 + core, y * 8 + k % 8)

    def row_device(k):
        return (dp, k)

    barrier = pltpu.get_barrier_semaphore()

    def greet(device, own_index, count):
        @pl.loop(1, count)
        def _(k):
            pl.semaphore_signal(
                barrier, inc=1, device_id=device((own_index + k) % count), device_id_type=MESH
            )

    greet(row_device, dap, 32)
    greet(plane_device, member, 32)
    greet(line_device, z, 16)

    def send(source, target, step, device):
        pltpu.make_async_remote_copy(
            src_ref=source,
            dst_ref=target,
            send_sem=sems.at[2 * step],
            recv_sem=sems.at[2 * step + 1],
            device_id=device,
            device_id_type=MESH,
        ).start()

    def wait_bytes(ref, semaphore):
        pltpu.make_async_copy(ref, ref, sems.at[semaphore]).wait()

    def exchange(source, landing, u, step):
        @pl.loop(1, 32)
        def _(k):
            d = (dap + k) % 32
            send(source.at[u, d], landing.at[u, dap], step + u, row_device(d))

        pltpu.make_async_copy(
            source.at[u, dap], landing.at[u, dap], sems.at[2 * (step + u) + 1]
        ).start()

    def arrive(landing, u, step):
        wait_bytes(landing.at[u], 2 * (step + u) + 1)

    def prepare():
        row = lax.broadcasted_iota(jnp.int32, (128, 128), 0)
        lane = lax.broadcasted_iota(jnp.int32, (128, 128), 1)
        by_device = (row & 3) * 32 + (row >> 4) * 4 + ((row >> 2) & 3)
        by_device_t = (lane & 3) * 32 + (lane >> 4) * 4 + ((lane >> 2) & 3)
        by_channel = ((row >> 2) & 7) * 16 + (row >> 5) * 4 + (row & 3)
        by_channel_t = ((lane >> 2) & 7) * 16 + (lane >> 5) * 4 + (lane & 3)
        perm[TO_OWNER] = jnp.where(lane == by_device, 1.0, 0.0).astype(BF16)
        perm[FROM_OWNER] = jnp.where(row == by_device_t, 1.0, 0.0).astype(BF16)
        perm[BY_CHANNEL] = jnp.where(lane == by_channel, 1.0, 0.0).astype(BF16)
        perm[BY_SOURCE] = jnp.where(row == by_channel_t, 1.0, 0.0).astype(BF16)

    def prepare_update(u):
        rows = [bias_ref[u : u + 1, 128 * g : 128 * (g + 1)] for g in range(5)]
        rows += [gain_ref[u : u + 1, 0:128], shift_ref[u : u + 1, 0:128]]
        rows += [gain_ref[u : u + 1, 128:256], shift_ref[u : u + 1, 128:256]]
        rows += [ob_ref[u : u + 1, :]]
        for k, values in enumerate(rows):
            col[u, k] = jnp.broadcast_to(values, (128, 128)).T
        for g in range(5):
            block = slice(128 * g, 128 * (g + 1))
            w_t[u, block, :] = transposed(w_ref[u, :, block])
        wo_t[u] = transposed(wo_ref[u])

    def project(u, r):
        unit, scale = normalise(state[u, r])
        values = (unit * col[u, GAIN_IN] + col[u, SHIFT_IN]).astype(BF16)
        unit_in[u, r] = unit
        scale_in[u, r] = scale
        normed[u, r] = values
        keep = mask_ref[pl.ds(r, 1), :].astype(F32)
        for side in range(2):
            g = 2 * side
            pre = dot(w_t[u, 128 * g : 128 * (g + 2), :], values)
            linear = pre[:128] + col[u, g]
            opened = sigmoid(pre[128:] + col[u, g + 1])
            edge[u, r, g] = linear
            edge[u, r, g + 1] = opened
            cm[r, :, 128 * side : 128 * (side + 1)] = (opened * linear * keep).astype(BF16)

    def open_gate(u, r):
        gate[u, r] = sigmoid(dot(w_t[u, 512:640, :], normed[u, r]) + col[u, 4])

    def pack(target, u, g, values, width):
        block = slice(8 * g, 8 * (g + 1))
        for side in range(width):
            target[u, block, 16 * side : 16 * (side + 1), :] = values[
                :, 128 * side : 128 * (side + 1)
            ].reshape(8, 16, 128)

    def unpack(landing, u, g, width):
        block = slice(8 * g, 8 * (g + 1))
        sides = [
            landing[u, block, 16 * side : 16 * (side + 1), :].reshape(128, 128)
            for side in range(width)
        ]
        return sides[0] if width == 1 else jnp.concatenate(sides, axis=1)

    def to_messages(source, which, target, u, width):
        def group(g):
            rows = slice(32 * g, 32 * (g + 1))
            block = jnp.concatenate(
                [source[q, rows, 0 : 128 * width] for q in range(4)], axis=0
            )
            pack(target, u, g, dot(perm[which], block).astype(BF16), width)

        each(4, group)

    def from_messages(landing, which, u, target, width):
        def group(g):
            values = dot(perm[which], unpack(landing, u, g, width)).astype(BF16)
            for q in range(4):
                target(q, slice(32 * g, 32 * (g + 1)), values[32 * q : 32 * (q + 1)])

        each(4, group)

    def store_own(u):
        def store(q, rows, values):
            own[u, q, rows, :] = values

        return store

    def store_out(q, rows, values):
        own_out[q, rows, 0:128] = values

    def store_cm(width):
        def store(q, rows, values):
            cm[q, rows, 0 : 128 * width] = values

        return store

    def multiply(u, h):
        left, right = own[u, h, :, 0:128], own[u, h, :, 128:256]
        if u == 0:
            values = dot_nt(left, right)
        else:
            values = dot(transposed(left), right)
        own_out[h, :, 0:128] = values.astype(BF16)

    def multiply_back(u, h):
        left, right = own[u, h, :, 0:128], own[u, h, :, 128:256]
        d_product = own_out[h, :, 0:128]
        if u == 0:
            d_left = dot(d_product, right)
            d_right = dot(transposed(d_product), left)
        else:
            d_left = dot_nt(right, d_product)
            d_right = dot(left, d_product)
        own_out[h, :, 0:128] = d_left.astype(BF16)
        own_out[h, :, 128:256] = d_right.astype(BF16)

    def mix(u, r):
        unit, scale = normalise(cm[r, :, 0:128].astype(F32))
        values = (unit * col[u, GAIN_OUT] + col[u, SHIFT_OUT]).astype(BF16)
        unit_out[u, r] = unit
        scale_out[u, r] = scale
        mixed[u, r] = values
        result = dot(wo_t[u], values) + col[u, OUT_BIAS]
        branch[u, r] = result
        if u == 0:
            state[1, r] = (state[0, r] + gate[0, r] * result).astype(BF16).astype(F32)

    def forward(u):
        each(4, lambda r: project(u, r))
        to_messages(cm, TO_OWNER, edge_send, u, 2)
        if u == 0:
            pl.semaphore_wait(barrier, 77)
        exchange(edge_send, edge_recv, u, EDGES)
        each(4, lambda r: open_gate(u, r))
        if u == 0:
            prepare_update(1)

            def load_cotangent(r):
                up[r] = cot_ref[r].astype(F32).T

            each(4, load_cotangent)
        arrive(edge_recv, u, EDGES)
        from_messages(edge_recv, BY_CHANNEL, u, store_own(u), 2)
        each(4, lambda h: multiply(u, h))
        to_messages(own_out, BY_SOURCE, prod_send, u, 1)
        exchange(prod_send, prod_recv, u, PRODUCTS)
        arrive(prod_recv, u, PRODUCTS)
        from_messages(prod_recv, FROM_OWNER, u, store_cm(1), 1)
        each(4, lambda r: mix(u, r))

    def branch_back(u, r):
        opened = gate[u, r]
        through = up[r] * opened
        values = through.astype(BF16)
        d_branch[r] = values
        d_edge[r, 512:640, :] = (through * branch[u, r] * (1.0 - opened)).astype(BF16)
        d_unit = dot(wo_ref[u], values) * col[u, GAIN_OUT]
        cm[r, :, 0:128] = norm_pullback(unit_out[u, r], scale_out[u, r], d_unit).astype(BF16)

    def edges_back(u, r):
        keep = mask_ref[pl.ds(r, 1), :].astype(F32)
        for side in range(2):
            g = 2 * side
            linear, opened = edge[u, r, g], edge[u, r, g + 1]
            through = cm[r, :, 128 * side : 128 * (side + 1)].astype(F32) * keep * opened
            d_edge[r, 128 * g : 128 * (g + 1), :] = through.astype(BF16)
            d_edge[r, 128 * (g + 1) : 128 * (g + 2), :] = (
                through * linear * (1.0 - opened)
            ).astype(BF16)

    def norm_back(u, r):
        d_unit = dot(w_ref[u], d_edge[r]) * col[u, GAIN_IN]
        result = up[r] + norm_pullback(unit_in[u, r], scale_in[u, r], d_unit)
        if u == 1:
            up[r] = result
        else:
            grad_ref[r] = result.T.astype(BF16)

    def proj_part(u, g):
        total = dot_nt(normed[u, 0], d_edge[0, 128 * g : 128 * (g + 1), :])
        for r in range(1, 4):
            total += dot_nt(normed[u, r], d_edge[r, 128 * g : 128 * (g + 1), :])
        return total.astype(BF16).reshape(8, 16, 128)

    def out_part(u):
        total = dot_nt(mixed[u, 0], d_branch[0])
        for r in range(1, 4):
            total += dot_nt(mixed[u, r], d_branch[r])
        return total.astype(BF16).reshape(8, 16, 128)

    def sum_step(unit, stage):
        return 8 + 3 * unit + stage

    def sum_begin(unit):
        step = sum_step(unit, 0)

        @pl.loop(1, 32)
        def _(k):
            j = (member + k) % 32
            send(sum_send.at[unit, j], plane_buf.at[unit, member], step, plane_device(j))

        pltpu.make_async_copy(
            sum_send.at[unit, member], plane_buf.at[unit, member], sems.at[2 * step + 1]
        ).start()

    def sum_line(unit):
        wait_bytes(plane_buf.at[unit], 2 * sum_step(unit, 0) + 1)
        z_send[unit] = jnp.sum(plane_buf[unit].astype(F32), axis=0).astype(BF16)
        step = sum_step(unit, 1)

        @pl.loop(1, 16)
        def _(k):
            send(z_send.at[unit], z_buf.at[unit, z], step, line_device((z + k) % 16))

        pltpu.make_async_copy(
            z_send.at[unit], z_buf.at[unit, z], sems.at[2 * step + 1]
        ).start()

    def sum_share(unit):
        wait_bytes(z_buf.at[unit], 2 * sum_step(unit, 1) + 1)
        own_total[unit] = jnp.sum(z_buf[unit].astype(F32), axis=0).astype(BF16)
        step = sum_step(unit, 2)

        @pl.loop(1, 32)
        def _(k):
            send(
                own_total.at[unit],
                all_buf.at[unit, member],
                step,
                plane_device((member + k) % 32),
            )

        pltpu.make_async_copy(
            own_total.at[unit], all_buf.at[unit, member], sems.at[2 * step + 1]
        ).start()

    def sum_end(unit):
        wait_bytes(all_buf.at[unit], 2 * sum_step(unit, 2) + 1)
        for g in range(4):
            values = all_buf[unit, 8 * g : 8 * (g + 1)].reshape(128, 128).astype(F32)
            if unit == 1:
                u = 1 - g // 2
                if g % 2 == 0:
                    proj_ref[u, :, 512:640] = values
                else:
                    out_ref[u] = values
            else:
                proj_ref[1 - unit // 2, :, 128 * g : 128 * (g + 1)] = values

    def backward(u):
        each(4, lambda r: branch_back(u, r))
        to_messages(cm, TO_OWNER, dprod_send, u, 1)
        exchange(dprod_send, dprod_recv, u, D_PRODUCTS)
        first = 0 if u == 1 else 16
        sum_send[1, first : first + 8] = proj_part(u, 4)
        sum_send[1, first + 8 : first + 16] = out_part(u)
        if u == 0:
            sum_begin(1)
            sum_line(0)
        arrive(dprod_recv, u, D_PRODUCTS)
        from_messages(dprod_recv, BY_CHANNEL, u, store_out, 1)
        each(4, lambda h: multiply_back(u, h))
        to_messages(own_out, BY_SOURCE, dedge_send, u, 2)
        exchange(dedge_send, dedge_recv, u, D_EDGES)
        if u == 0:
            sum_share(0)
            sum_line(1)
        arrive(dedge_recv, u, D_EDGES)
        from_messages(dedge_recv, FROM_OWNER, u, store_cm(2), 2)
        each(4, lambda r: edges_back(u, r))
        unit = 0 if u == 1 else 2
        for g in range(4):
            sum_send[unit, 8 * g : 8 * (g + 1)] = proj_part(u, g)
        sum_begin(unit)
        each(4, lambda r: norm_back(u, r))

    prepare()
    prepare_update(0)

    def load_state(r):
        state[0, r] = pair_ref[r].astype(F32).T

    each(4, load_state)
    forward(0)
    forward(1)
    backward(1)
    backward(0)
    sum_share(1)
    sum_line(2)
    sum_end(0)
    sum_share(2)
    sum_end(1)
    sum_end(2)
    for step, sent in (
        (EDGES, edge_send),
        (PRODUCTS, prod_send),
        (D_PRODUCTS, dprod_send),
        (D_EDGES, dedge_send),
    ):
        for u in range(2):
            wait_bytes(sent.at[u, pl.ds(0, 31)], 2 * (step + u))
    for unit in range(3):
        wait_bytes(plane_buf.at[unit, pl.ds(0, 31)], 2 * sum_step(unit, 0))
        wait_bytes(z_buf.at[unit, pl.ds(0, 15)], 2 * sum_step(unit, 1))
        wait_bytes(all_buf.at[unit, pl.ds(0, 31)], 2 * sum_step(unit, 2))


def shards(
    pair_repr,
    pair_mask,
    cotangent,
    proj_weight,
    proj_bias,
    norm_gain,
    norm_shift,
    out_weight,
    out_bias,
):
    def real(*shape):
        return pltpu.VMEM(shape, F32)

    def half(*shape):
        return pltpu.VMEM(shape, BF16)

    vmem = pl.BlockSpec(memory_space=pltpu.VMEM)
    pair_grad, proj_grad, out_grad = pl.pallas_call(
        kernel,
        out_shape=(
            jax.ShapeDtypeStruct((4, 128, 128), BF16),
            jax.ShapeDtypeStruct((2, 128, 640), F32),
            jax.ShapeDtypeStruct((2, 128, 128), F32),
        ),
        in_specs=[vmem] * 9,
        out_specs=(vmem, vmem, vmem),
        scratch_shapes=[
            half(2, 640, 128),
            half(2, 128, 128),
            half(4, 128, 128),
            real(2, 10, 128, 128),
            real(2, 4, 128, 128),
            half(2, 4, 128, 128),
            real(2, 4, 128, 128),
            real(2, 4, 1, 128),
            real(2, 4, 4, 128, 128),
            real(2, 4, 128, 128),
            real(2, 4, 128, 128),
            real(2, 4, 128, 128),
            real(2, 4, 1, 128),
            half(2, 4, 128, 128),
            real(4, 128, 128),
            half(4, 640, 128),
            half(4, 128, 128),
            half(4, 128, 256),
            half(2, 4, 128, 256),
            half(4, 128, 256),
            half(2, 32, 32, 128),
            half(2, 32, 32, 128),
            half(2, 32, 16, 128),
            half(2, 32, 16, 128),
            half(2, 32, 16, 128),
            half(2, 32, 16, 128),
            half(2, 32, 32, 128),
            half(2, 32, 32, 128),
            half(3, 32, 16, 128),
            half(3, 32, 16, 128),
            half(3, 16, 128),
            half(3, 16, 16, 128),
            half(3, 16, 128),
            half(3, 32, 16, 128),
            pltpu.SemaphoreType.DMA((34,)),
        ],
        compiler_params=pltpu.CompilerParams(
            collective_id=1, has_side_effects=True, vmem_limit_bytes=40 << 20
        ),
    )(
        pair_repr[0],
        pair_mask[0],
        cotangent[0],
        proj_weight,
        proj_bias,
        norm_gain,
        norm_shift,
        out_weight,
        out_bias,
    )
    return pair_grad[None], proj_grad, out_grad


def solution(mesh):
    placed = (
        P("dp", "dap", None, None),
        P("dp", "dap", None),
        P("dp", "dap", None, None),
        P(),
        P(),
        P(),
        P(),
        P(),
        P(),
    )
    return jax.shard_map(
        shards,
        mesh=mesh,
        in_specs=placed,
        out_specs=(P("dp", "dap", None, None), P(), P()),
        check_vma=False,
    )
```

time: 694 us -> 147 us (0.21)
  waiting for transfers between devices: 509 us -> 0 us
  Pallas kernels: 0 us -> 137 us
  blocking collectives: 94.8 us -> 0 us
  local copies, waits for them, and re-layouts: 36.5 us -> 9.17 us
  starting transfers between devices: 23.5 us -> 0 us
  between operations: 15.1 us -> 0.66 us
  matrix products: 8.93 us -> 0 us
    psum x1 -> x0, waiting for transfers between devices: 462 us -> none  [shards(): proj_total, out_total = lax.psum((proj_total, out_total), ('dp', 'dap'))]
    pallas_call x0 -> x1, Pallas kernels: none -> 137 us  [shards(): pl.pallas_call(kernel, out_shape=(jax.ShapeDtypeStruct((4, 128, 128), BF1...]
    all_to_all x4 -> x0, blocking collectives: 94.8 us -> none  [the longest x2 59.9 us: shards(): lax.all_to_all(pair_edges, 'dap', split_axis=1, concat_axis=2, tiled=True)]
    all_to_all x4 -> x0, waiting for transfers between devices: 46.9 us -> none  [the longest x2 26.7 us: shards(): lax.all_to_all(triangle_pullback(column_edges, column_grad, update == 0),...]
    all_to_all x4 -> x0, starting transfers between devices: 23.5 us -> none  [the longest x2 12.8 us: shards(): lax.all_to_all(triangle_pullback(column_edges, column_grad, update == 0),...]
    unnamed x172 -> x21, local copies, waits for them, and re-layouts: 26.7 us -> 9.17 us
    dot_general x24 -> x0, matrix products: 8.93 us -> none  [the longest x2 2.11 us: shards(): jnp.einsum('rnc,cd->rnd', normed, w_gate, preferred_element_type=jnp.floa...]
  transfers between devices with their start and end apart: 5 -> 0, of which waited for: 5 -> 0; matrix products, arithmetic and copies ran while one was open for 1% -> 0% of each run, Pallas kernels for 0% -> 0%
where the time goes in v2:
time: 147 us
  Pallas kernels  137 us (93%)
  local copies, waits for them, and re-layouts  9.17 us (6%)
    pallas_call x1, Pallas kernels, shards(): pl.pallas_call(kernel, out_shape=(jax.ShapeDtypeStruct((4, 128, 128), BF1...  137 us
    unnamed x21, local copies, waits for them, and re-layouts  9.17 us

profile of v2, /device:TPU:1, one launch (start us, length us, event | category | flops | bytes accessed | tf_op | source)
XLA Modules:
  0.0 147.0 jit_solution(6594624644394098480)
XLA Ops:
  0.6 0.0 copy-start.4
  0.6 0.7 copy-done.4
  1.3 0.0 copy-start
  1.3 1.0 copy-done
  2.3 0.0 copy-start.1
  2.3 0.9 copy-done.1
  3.2 0.0 copy-start.2
  3.2 0.9 copy-done.2
  4.1 0.0 copy-start.3
  4.1 0.8 copy-done.3
  4.9 0.0 copy-start.5
  4.9 0.7 copy-done.5
  5.6 0.0 copy-start.6
  5.6 0.7 copy-done.6
  6.3 0.0 copy-start.7
  6.3 0.7 copy-done.7
  7.0 0.0 copy-start.8
  7.0 0.7 copy-done.8
  7.7 137.2 %shard_map.112 = (bf16[4,128,128]{2,1,0:T(8,128)(2,1)S(1)}, f32[2,128,640]{2,1,0:T(8,128)S(1)}, f32[2,128,128]{2,1,0:T(8,128)S(1)}) custom-call(bf16[4,128,128]{2,1,0:T(8,128)(2,1)S(1)} %bitcast.5, s32[4,128]{1,0:T(4,128)S(1)} %bitcast.7, bf16[4,128,128]{2,1,0:T(8,128)(2,1)S(1)} %bitcast.6, bf16[2,128,640]{2,1,0:T(8,128)(2,1)S(1)} %copy-done, ...), custom_call_target="tpu_custom_call" | custom-call | tf_op jit(solution)/shard_map/pallas_call | solution.py:476
  144.8 0.7 copy.15
  145.5 0.8 copy.16
  146.3 0.7 copy.17
Async XLA Ops:
  0.6 0.7 copy-start.4
  1.3 1.0 copy-start
  2.3 0.9 copy-start.1
  3.2 0.9 copy-start.2
  4.1 0.8 copy-start.3
  4.9 0.7 copy-start.5
  5.6 0.7 copy-start.6
  6.3 0.7 copy-start.7
  7.0 0.7 copy-start.8

commit v3 on v2

--- a/solution.py
+++ b/solution.py
@@ -12,6 +12,7 @@
 EDGES, PRODUCTS, D_PRODUCTS, D_EDGES = 0, 2, 4, 6
 GAIN_IN, SHIFT_IN, GAIN_OUT, SHIFT_OUT, OUT_BIAS = 5, 6, 7, 8, 9
 TO_OWNER, FROM_OWNER, BY_CHANNEL, BY_SOURCE = 0, 1, 2, 3
+LOADS, PAIR_SENT, PAIR_CAME, MASK_MOVE, COT_MOVE, GRAD_SENT, GRAD_CAME = 34, 40, 41, 45, 47, 49, 50
 
 
 def dot(a, b):
@@ -50,18 +51,29 @@
 
 
 def kernel(
-    pair_ref,
-    mask_ref,
-    cot_ref,
+    pair_in,
+    mask_in,
+    cot_in,
+    w_in,
+    bias_in,
+    gain_in,
+    shift_in,
+    wo_in,
+    ob_in,
+    grad_ref,
+    proj_ref,
+    out_ref,
     w_ref,
     bias_ref,
     gain_ref,
     shift_ref,
     wo_ref,
     ob_ref,
-    grad_ref,
-    proj_ref,
-    out_ref,
+    mask_ref,
+    pair_buf,
+    cot_buf,
+    grad_send,
+    grad_buf,
     w_t,
     wo_t,
     perm,
@@ -102,17 +114,26 @@
     dap = lax.axis_index("dap")
     core, z_hi, x = dp % 2, (dp // 2) % 2, dp // 4
     y, z_lo = dap // 8, dap % 8
-    member = (x * 4 + y) * 2 + core
+    home_x = z_lo % 4
+    member = y * 8 + core * 4 + x
+    slot = y * 8 + core * 4 + (x + 4 - home_x) % 4
     z = z_hi * 8 + z_lo
 
-    def plane_device(j):
-        return ((j // 8) * 4 + z_hi * 2 + j % 2, ((j // 2) % 4) * 8 + z_lo)
+    def member_device(k):
+        return ((k % 4) * 4 + z_hi * 2 + (k // 4) % 2, (k // 8) * 8 + z_lo)
+
+    def slot_device(k):
+        return (((k + home_x) % 4) * 4 + z_hi * 2 + (k // 4) % 2, (k // 8) * 8 + z_lo)
 
     def line_device(k):
         return (x * 4 + (k // 8) * 2 + core, y * 8 + k % 8)
 
-    def row_device(k):
-        return (dp, k)
+    worker = (((z_lo + x) % 4) * 4 + z_hi * 2 + z_lo // 4, y * 8 + core * 4 + x)
+    home = (
+        home_x * 4 + z_hi * 2 + z_lo // 4,
+        slot,
+    )
+    away = (worker[0] != dp) | (worker[1] != dap)
 
     barrier = pltpu.get_barrier_semaphore()
 
@@ -123,8 +144,12 @@
                 barrier, inc=1, device_id=device((own_index + k) % count), device_id_type=MESH
             )
 
-    greet(row_device, dap, 32)
-    greet(plane_device, member, 32)
+    @pl.when(away)
+    def _():
+        pl.semaphore_signal(barrier, inc=1, device_id=worker, device_id_type=MESH)
+        pl.semaphore_signal(barrier, inc=1, device_id=home, device_id_type=MESH)
+
+    greet(member_device, member, 32)
     greet(line_device, z, 16)
 
     def send(source, target, step, device):
@@ -140,18 +165,39 @@
     def wait_bytes(ref, semaphore):
         pltpu.make_async_copy(ref, ref, sems.at[semaphore]).wait()
 
+    def far_first(k):
+        order = 32 - k
+        x_rank, y_rank = (order // 2) % 4, order // 8
+        return (x_rank ^ (x_rank // 2)) + (order % 2) * 4 + (y_rank ^ (y_rank // 2)) * 8
+
     def exchange(source, landing, u, step):
         @pl.loop(1, 32)
         def _(k):
-            d = (dap + k) % 32
-            send(source.at[u, d], landing.at[u, dap], step + u, row_device(d))
+            d = slot ^ far_first(k)
+            send(source.at[u, d], landing.at[u, slot], step + u, slot_device(d))
 
         pltpu.make_async_copy(
-            source.at[u, dap], landing.at[u, dap], sems.at[2 * (step + u) + 1]
+            source.at[u, slot], landing.at[u, slot], sems.at[2 * (step + u) + 1]
         ).start()
 
     def arrive(landing, u, step):
         wait_bytes(landing.at[u], 2 * (step + u) + 1)
+
+    def move(source, target, sent, came, device):
+        @pl.when(away)
+        def _():
+            pltpu.make_async_remote_copy(
+                src_ref=source,
+                dst_ref=target,
+                send_sem=sems.at[sent],
+                recv_sem=sems.at[came],
+                device_id=device,
+                device_id_type=MESH,
+            ).start()
+
+        @pl.when(jnp.logical_not(away))
+        def _():
+            pltpu.make_async_copy(source, target, sems.at[came]).start()
 
     def prepare():
         row = lax.broadcasted_iota(jnp.int32, (128, 128), 0)
@@ -276,17 +322,23 @@
             state[1, r] = (state[0, r] + gate[0, r] * result).astype(BF16).astype(F32)
 
     def forward(u):
-        each(4, lambda r: project(u, r))
+        if u == 0:
+            for r in range(4):
+                wait_bytes(pair_buf.at[r], PAIR_CAME + r)
+                state[0, r] = pair_buf[r].astype(F32).T
+                project(0, r)
+        else:
+            each(4, lambda r: project(u, r))
         to_messages(cm, TO_OWNER, edge_send, u, 2)
-        if u == 0:
-            pl.semaphore_wait(barrier, 77)
         exchange(edge_send, edge_recv, u, EDGES)
         each(4, lambda r: open_gate(u, r))
         if u == 0:
-            prepare_update(1)
+            move(cot_in, cot_buf, COT_MOVE, COT_MOVE + 1, worker)
+        else:
+            wait_bytes(cot_buf, COT_MOVE + 1)
 
             def load_cotangent(r):
-                up[r] = cot_ref[r].astype(F32).T
+                up[r] = cot_buf[r].astype(F32).T
 
             each(4, load_cotangent)
         arrive(edge_recv, u, EDGES)
@@ -324,7 +376,8 @@
         if u == 1:
             up[r] = result
         else:
-            grad_ref[r] = result.T.astype(BF16)
+            grad_send[r] = result.T.astype(BF16)
+            move(grad_send.at[r], grad_buf.at[r], GRAD_SENT, GRAD_CAME, home)
 
     def proj_part(u, g):
         total = dot_nt(normed[u, 0], d_edge[0, 128 * g : 128 * (g + 1), :])
@@ -346,8 +399,8 @@
 
         @pl.loop(1, 32)
         def _(k):
-            j = (member + k) % 32
-            send(sum_send.at[unit, j], plane_buf.at[unit, member], step, plane_device(j))
+            j = member ^ far_first(k)
+            send(sum_send.at[unit, j], plane_buf.at[unit, member], step, member_device(j))
 
         pltpu.make_async_copy(
             sum_send.at[unit, member], plane_buf.at[unit, member], sems.at[2 * step + 1]
@@ -360,7 +413,7 @@
 
         @pl.loop(1, 16)
         def _(k):
-            send(z_send.at[unit], z_buf.at[unit, z], step, line_device((z + k) % 16))
+            send(z_send.at[unit], z_buf.at[unit, z], step, line_device(z ^ k))
 
         pltpu.make_async_copy(
             z_send.at[unit], z_buf.at[unit, z], sems.at[2 * step + 1]
@@ -377,7 +430,7 @@
                 own_total.at[unit],
                 all_buf.at[unit, member],
                 step,
-                plane_device((member + k) % 32),
+                member_device(member ^ far_first(k)),
             )
 
         pltpu.make_async_copy(
@@ -424,13 +477,32 @@
         sum_begin(unit)
         each(4, lambda r: norm_back(u, r))
 
+    loads = [
+        pltpu.make_async_copy(source, target, sems.at[LOADS + k])
+        for k, (source, target) in enumerate(
+            (
+                (w_in, w_ref),
+                (bias_in, bias_ref),
+                (gain_in, gain_ref),
+                (shift_in, shift_ref),
+                (wo_in, wo_ref),
+                (ob_in, ob_ref),
+            )
+        )
+    ]
+    for load in loads:
+        load.start()
+    pl.semaphore_wait(barrier, jnp.where(away, 48, 46))
+
+    move(mask_in, mask_ref, MASK_MOVE, MASK_MOVE + 1, worker)
+    for r in range(4):
+        move(pair_in.at[r], pair_buf.at[r], PAIR_SENT, PAIR_CAME + r, worker)
+    for load in loads:
+        load.wait()
     prepare()
     prepare_update(0)
-
-    def load_state(r):
-        state[0, r] = pair_ref[r].astype(F32).T
-
-    each(4, load_state)
+    prepare_update(1)
+    wait_bytes(mask_ref, MASK_MOVE + 1)
     forward(0)
     forward(1)
     backward(1)
@@ -441,6 +513,16 @@
     sum_share(2)
     sum_end(1)
     sum_end(2)
+    wait_bytes(grad_buf, GRAD_CAME)
+    grad_ref[...] = grad_buf[...]
+
+    @pl.when(away)
+    def _():
+        wait_bytes(pair_buf, PAIR_SENT)
+        wait_bytes(mask_ref, MASK_MOVE)
+        wait_bytes(cot_buf, COT_MOVE)
+        wait_bytes(grad_buf, GRAD_SENT)
+
     for step, sent in (
         (EDGES, edge_send),
         (PRODUCTS, prod_send),
@@ -480,9 +562,20 @@
             jax.ShapeDtypeStruct((2, 128, 640), F32),
             jax.ShapeDtypeStruct((2, 128, 128), F32),
         ),
-        in_specs=[vmem] * 9,
+        in_specs=[pl.BlockSpec(memory_space=pl.ANY)] * 9,
         out_specs=(vmem, vmem, vmem),
         scratch_shapes=[
+            half(2, 128, 640),
+            real(2, 640),
+            real(2, 256),
+            real(2, 256),
+            half(2, 128, 128),
+            real(2, 128),
+            pltpu.VMEM((4, 128), jnp.int32),
+            half(4, 128, 128),
+            half(4, 128, 128),
+            half(4, 128, 128),
+            half(4, 128, 128),
             half(2, 640, 128),
             half(2, 128, 128),
             half(4, 128, 128),
@@ -517,7 +610,7 @@
             half(3, 16, 16, 128),
             half(3, 16, 128),
             half(3, 32, 16, 128),
-            pltpu.SemaphoreType.DMA((34,)),
+            pltpu.SemaphoreType.DMA((51,)),
         ],
         compiler_params=pltpu.CompilerParams(
             collective_id=1, has_side_effects=True, vmem_limit_bytes=40 << 20

time: 147 us -> 117 us (0.80)
  Pallas kernels: 137 us -> 106 us
    pallas_call x1, Pallas kernels: 137 us -> 106 us  [shards(): pl.pallas_call(kernel, out_shape=(jax.ShapeDtypeStruct((4, 128, 128), BF1...]
where the time goes in v3:
time: 117 us; the launch traced here: 116 us
  Pallas kernels  106 us (91%)
  local copies, waits for them, and re-layouts  9.17 us (8%)
    pallas_call x1, Pallas kernels, shards(): pl.pallas_call(kernel, out_shape=(jax.ShapeDtypeStruct((4, 128, 128), BF1...  106 us
    unnamed x21, local copies, waits for them, and re-layouts  9.17 us

profile of v3, /device:TPU:1, one launch (start us, length us, event | category | flops | bytes accessed | tf_op | source)
XLA Modules:
  0.0 116.2 jit_solution(15017385996390711157)
XLA Ops:
  0.6 0.0 copy-start.4
  0.6 0.7 copy-done.4
  1.3 0.0 copy-start
  1.3 1.0 copy-done
  2.3 0.0 copy-start.1
  2.3 0.9 copy-done.1
  3.2 0.0 copy-start.2
  3.2 0.9 copy-done.2
  4.1 0.0 copy-start.3
  4.1 0.8 copy-done.3
  4.9 0.0 copy-start.5
  4.9 0.7 copy-done.5
  5.6 0.0 copy-start.6
  5.6 0.7 copy-done.6
  6.3 0.0 copy-start.7
  6.3 0.7 copy-done.7
  7.0 0.0 copy-start.8
  7.0 0.7 copy-done.8
  7.7 106.3 %shard_map.112 = (bf16[4,128,128]{2,1,0:T(8,128)(2,1)S(1)}, f32[2,128,640]{2,1,0:T(8,128)S(1)}, f32[2,128,128]{2,1,0:T(8,128)S(1)}) custom-call(bf16[4,128,128]{2,1,0:T(8,128)(2,1)S(1)} %bitcast.5, s32[4,128]{1,0:T(4,128)S(1)} %bitcast.7, bf16[4,128,128]{2,1,0:T(8,128)(2,1)S(1)} %bitcast.6, bf16[2,128,640]{2,1,0:T(8,128)(2,1)S(1)} %copy-done, ...), custom_call_target="tpu_custom_call" | custom-call | tf_op jit(solution)/shard_map/pallas_call | solution.py:558
  114.0 0.7 copy.15
  114.7 0.8 copy.16
  115.5 0.7 copy.17
Async XLA Ops:
  0.6 0.7 copy-start.4
  1.3 1.0 copy-start
  2.3 0.9 copy-start.1
  3.2 0.9 copy-start.2
  4.1 0.8 copy-start.3
  4.9 0.7 copy-start.5
  5.6 0.7 copy-start.6
  6.3 0.7 copy-start.7
  7.0 0.7 copy-start.8

commit v4 on v3

--- a/solution.py
+++ b/solution.py
@@ -12,7 +12,9 @@
 EDGES, PRODUCTS, D_PRODUCTS, D_EDGES = 0, 2, 4, 6
 GAIN_IN, SHIFT_IN, GAIN_OUT, SHIFT_OUT, OUT_BIAS = 5, 6, 7, 8, 9
 TO_OWNER, FROM_OWNER, BY_CHANNEL, BY_SOURCE = 0, 1, 2, 3
-LOADS, PAIR_SENT, PAIR_CAME, MASK_MOVE, COT_MOVE, GRAD_SENT, GRAD_CAME = 34, 40, 41, 45, 47, 49, 50
+RECEIVED, EARLY, LATE, LOADS, PAIR_SENT, PAIR_CAME = 8, 40, 46, 52, 58, 59
+MASK_MOVE, COT_MOVE, GRAD_SENT, GRAD_CAME, SEMAPHORES = 63, 65, 67, 68, 69
+FAR_FIRST = (2, 3, 1, 0)
 
 
 def dot(a, b):
@@ -102,35 +104,43 @@
     dprod_recv,
     dedge_send,
     dedge_recv,
-    sum_send,
-    plane_buf,
-    z_send,
-    z_buf,
-    own_total,
-    all_buf,
+    early_part,
+    early_planes,
+    early_own,
+    early_lines,
+    early_sum,
+    early_totals,
+    late_part,
+    late_planes,
+    late_own,
+    late_lines,
+    late_sum,
+    late_totals,
     sems,
 ):
+    early = (early_part, early_planes, early_own, early_lines, early_sum, early_totals)
+    late = (late_part, late_planes, late_own, late_lines, late_sum, late_totals)
     dp = lax.axis_index("dp")
     dap = lax.axis_index("dap")
-    core, z_hi, x = dp % 2, (dp // 2) % 2, dp // 4
-    y, z_lo = dap // 8, dap % 8
-    home_x = z_lo % 4
+    core, z_hi, x = dp & 1, (dp >> 1) & 1, dp >> 2
+    y, z_lo = dap >> 3, dap & 7
+    home_x = z_lo & 3
     member = y * 8 + core * 4 + x
-    slot = y * 8 + core * 4 + (x + 4 - home_x) % 4
+    slot = y * 8 + core * 4 + ((x + 4 - home_x) & 3)
     z = z_hi * 8 + z_lo
 
     def member_device(k):
-        return ((k % 4) * 4 + z_hi * 2 + (k // 4) % 2, (k // 8) * 8 + z_lo)
+        return ((k & 3) * 4 + z_hi * 2 + ((k >> 2) & 1), (k >> 3) * 8 + z_lo)
 
     def slot_device(k):
-        return (((k + home_x) % 4) * 4 + z_hi * 2 + (k // 4) % 2, (k // 8) * 8 + z_lo)
+        return (((k + home_x) & 3) * 4 + z_hi * 2 + ((k >> 2) & 1), (k >> 3) * 8 + z_lo)
 
     def line_device(k):
-        return (x * 4 + (k // 8) * 2 + core, y * 8 + k % 8)
-
-    worker = (((z_lo + x) % 4) * 4 + z_hi * 2 + z_lo // 4, y * 8 + core * 4 + x)
+        return (x * 4 + (k >> 3) * 2 + core, y * 8 + (k & 7))
+
+    worker = (((z_lo + x) & 3) * 4 + z_hi * 2 + (z_lo >> 2), y * 8 + core * 4 + x)
     home = (
-        home_x * 4 + z_hi * 2 + z_lo // 4,
+        home_x * 4 + z_hi * 2 + (z_lo >> 2),
         slot,
     )
     away = (worker[0] != dp) | (worker[1] != dap)
@@ -141,7 +151,7 @@
         @pl.loop(1, count)
         def _(k):
             pl.semaphore_signal(
-                barrier, inc=1, device_id=device((own_index + k) % count), device_id_type=MESH
+                barrier, inc=1, device_id=device((own_index + k) & (count - 1)), device_id_type=MESH
             )
 
     @pl.when(away)
@@ -152,12 +162,12 @@
     greet(member_device, member, 32)
     greet(line_device, z, 16)
 
-    def send(source, target, step, device):
+    def send(source, target, sent, received, device):
         pltpu.make_async_remote_copy(
             src_ref=source,
             dst_ref=target,
-            send_sem=sems.at[2 * step],
-            recv_sem=sems.at[2 * step + 1],
+            send_sem=sems.at[sent],
+            recv_sem=sems.at[received],
             device_id=device,
             device_id_type=MESH,
         ).start()
@@ -167,21 +177,27 @@
 
     def far_first(k):
         order = 32 - k
-        x_rank, y_rank = (order // 2) % 4, order // 8
-        return (x_rank ^ (x_rank // 2)) + (order % 2) * 4 + (y_rank ^ (y_rank // 2)) * 8
-
-    def exchange(source, landing, u, step):
-        @pl.loop(1, 32)
+        x_rank, y_rank = (order >> 1) & 3, order >> 3
+        return (x_rank ^ (x_rank >> 1)) | ((order & 1) << 2) | ((y_rank ^ (y_rank >> 1)) << 3)
+
+    def exchange_group(source, landing, u, step, apart):
+        group = y ^ apart
+        received = RECEIVED + 4 * (step + u) + y
+
+        @pl.loop(0, 7 if apart == 0 else 8)
         def _(k):
-            d = slot ^ far_first(k)
-            send(source.at[u, d], landing.at[u, slot], step + u, slot_device(d))
-
-        pltpu.make_async_copy(
-            source.at[u, slot], landing.at[u, slot], sems.at[2 * (step + u) + 1]
-        ).start()
-
-    def arrive(landing, u, step):
-        wait_bytes(landing.at[u], 2 * (step + u) + 1)
+            order = 7 - k
+            x_rank = order >> 1
+            offset = (x_rank ^ (x_rank >> 1)) | ((order & 1) << 2)
+            d = group * 8 + ((slot & 7) ^ offset)
+            send(
+                source.at[u, d], landing.at[u, slot], step + u, received, slot_device(d)
+            )
+
+        if apart == 0:
+            pltpu.make_async_copy(
+                source.at[u, slot], landing.at[u, slot], sems.at[received]
+            ).start()
 
     def move(source, target, sent, came, device):
         @pl.when(away)
@@ -242,38 +258,42 @@
     def open_gate(u, r):
         gate[u, r] = sigmoid(dot(w_t[u, 512:640, :], normed[u, r]) + col[u, 4])
 
-    def pack(target, u, g, values, width):
-        block = slice(8 * g, 8 * (g + 1))
+    def pack(target, u, block, values, width):
         for side in range(width):
             target[u, block, 16 * side : 16 * (side + 1), :] = values[
                 :, 128 * side : 128 * (side + 1)
             ].reshape(8, 16, 128)
 
-    def unpack(landing, u, g, width):
-        block = slice(8 * g, 8 * (g + 1))
+    def unpack(landing, u, block, width):
         sides = [
             landing[u, block, 16 * side : 16 * (side + 1), :].reshape(128, 128)
             for side in range(width)
         ]
         return sides[0] if width == 1 else jnp.concatenate(sides, axis=1)
 
-    def to_messages(source, which, target, u, width):
-        def group(g):
-            rows = slice(32 * g, 32 * (g + 1))
-            block = jnp.concatenate(
+    def group_slices(apart):
+        group = y ^ apart
+        return (
+            pl.ds(pl.multiple_of(group * 8, 8), 8),
+            pl.ds(pl.multiple_of(group * 32, 32), 32),
+        )
+
+    def send_messages(source, which, target, landing, u, step, width):
+        for apart in FAR_FIRST:
+            block, rows = group_slices(apart)
+            values = jnp.concatenate(
                 [source[q, rows, 0 : 128 * width] for q in range(4)], axis=0
             )
-            pack(target, u, g, dot(perm[which], block).astype(BF16), width)
-
-        each(4, group)
-
-    def from_messages(landing, which, u, target, width):
-        def group(g):
-            values = dot(perm[which], unpack(landing, u, g, width)).astype(BF16)
+            pack(target, u, block, dot(perm[which], values).astype(BF16), width)
+            exchange_group(target, landing, u, step, apart)
+
+    def take_messages(landing, which, u, step, target, width):
+        for apart in FAR_FIRST:
+            block, rows = group_slices(apart)
+            wait_bytes(landing.at[u, block], RECEIVED + 4 * (step + u) + (y ^ apart))
+            values = dot(perm[which], unpack(landing, u, block, width)).astype(BF16)
             for q in range(4):
-                target(q, slice(32 * g, 32 * (g + 1)), values[32 * q : 32 * (q + 1)])
-
-        each(4, group)
+                target(q, rows, values[32 * q : 32 * (q + 1)])
 
     def store_own(u):
         def store(q, rows, values):
@@ -329,8 +349,7 @@
                 project(0, r)
         else:
             each(4, lambda r: project(u, r))
-        to_messages(cm, TO_OWNER, edge_send, u, 2)
-        exchange(edge_send, edge_recv, u, EDGES)
+        send_messages(cm, TO_OWNER, edge_send, edge_recv, u, EDGES, 2)
         each(4, lambda r: open_gate(u, r))
         if u == 0:
             move(cot_in, cot_buf, COT_MOVE, COT_MOVE + 1, worker)
@@ -341,13 +360,10 @@
                 up[r] = cot_buf[r].astype(F32).T
 
             each(4, load_cotangent)
-        arrive(edge_recv, u, EDGES)
-        from_messages(edge_recv, BY_CHANNEL, u, store_own(u), 2)
+        take_messages(edge_recv, BY_CHANNEL, u, EDGES, store_own(u), 2)
         each(4, lambda h: multiply(u, h))
-        to_messages(own_out, BY_SOURCE, prod_send, u, 1)
-        exchange(prod_send, prod_recv, u, PRODUCTS)
-        arrive(prod_recv, u, PRODUCTS)
-        from_messages(prod_recv, FROM_OWNER, u, store_cm(1), 1)
+        send_messages(own_out, BY_SOURCE, prod_send, prod_recv, u, PRODUCTS, 1)
+        take_messages(prod_recv, FROM_OWNER, u, PRODUCTS, store_cm(1), 1)
         each(4, lambda r: mix(u, r))
 
     def branch_back(u, r):
@@ -377,105 +393,121 @@
             up[r] = result
         else:
             grad_send[r] = result.T.astype(BF16)
-            move(grad_send.at[r], grad_buf.at[r], GRAD_SENT, GRAD_CAME, home)
+
+    def send_grad(r):
+        move(grad_send.at[r], grad_buf.at[r], GRAD_SENT, GRAD_CAME, home)
 
     def proj_part(u, g):
         total = dot_nt(normed[u, 0], d_edge[0, 128 * g : 128 * (g + 1), :])
         for r in range(1, 4):
             total += dot_nt(normed[u, r], d_edge[r, 128 * g : 128 * (g + 1), :])
-        return total.astype(BF16).reshape(8, 16, 128)
+        return total.astype(BF16)
 
     def out_part(u):
         total = dot_nt(mixed[u, 0], d_branch[0])
         for r in range(1, 4):
             total += dot_nt(mixed[u, r], d_branch[r])
-        return total.astype(BF16).reshape(8, 16, 128)
-
-    def sum_step(unit, stage):
-        return 8 + 3 * unit + stage
-
-    def sum_begin(unit):
-        step = sum_step(unit, 0)
+        return total.astype(BF16)
+
+    def begin_sum(unit, step):
+        part, planes = unit[0], unit[1]
 
         @pl.loop(1, 32)
         def _(k):
             j = member ^ far_first(k)
-            send(sum_send.at[unit, j], plane_buf.at[unit, member], step, member_device(j))
-
-        pltpu.make_async_copy(
-            sum_send.at[unit, member], plane_buf.at[unit, member], sems.at[2 * step + 1]
-        ).start()
-
-    def sum_line(unit):
-        wait_bytes(plane_buf.at[unit], 2 * sum_step(unit, 0) + 1)
-        z_send[unit] = jnp.sum(plane_buf[unit].astype(F32), axis=0).astype(BF16)
-        step = sum_step(unit, 1)
+            send(part.at[j], planes.at[member], step, step + 1, member_device(j))
+
+        pltpu.make_async_copy(part.at[member], planes.at[member], sems.at[step + 1]).start()
+
+    def sum_line(unit, step):
+        planes, own_part, lines = unit[1], unit[2], unit[3]
+        wait_bytes(planes, step + 1)
+        own_part[...] = jnp.sum(planes[...].astype(F32), axis=0).astype(BF16)
 
         @pl.loop(1, 16)
         def _(k):
-            send(z_send.at[unit], z_buf.at[unit, z], step, line_device(z ^ k))
-
-        pltpu.make_async_copy(
-            z_send.at[unit], z_buf.at[unit, z], sems.at[2 * step + 1]
-        ).start()
-
-    def sum_share(unit):
-        wait_bytes(z_buf.at[unit], 2 * sum_step(unit, 1) + 1)
-        own_total[unit] = jnp.sum(z_buf[unit].astype(F32), axis=0).astype(BF16)
-        step = sum_step(unit, 2)
+            send(own_part, lines.at[z], step + 2, step + 3, line_device(z ^ k))
+
+        pltpu.make_async_copy(own_part, lines.at[z], sems.at[step + 3]).start()
+
+    def share_sum(unit, step):
+        lines, own_total, totals = unit[3], unit[4], unit[5]
+        wait_bytes(lines, step + 3)
+        own_total[...] = jnp.sum(lines[...].astype(F32), axis=0).astype(BF16)
 
         @pl.loop(1, 32)
         def _(k):
             send(
-                own_total.at[unit],
-                all_buf.at[unit, member],
-                step,
+                own_total,
+                totals.at[member],
+                step + 4,
+                step + 5,
                 member_device(member ^ far_first(k)),
             )
 
-        pltpu.make_async_copy(
-            own_total.at[unit], all_buf.at[unit, member], sems.at[2 * step + 1]
-        ).start()
-
-    def sum_end(unit):
-        wait_bytes(all_buf.at[unit], 2 * sum_step(unit, 2) + 1)
+        pltpu.make_async_copy(own_total, totals.at[member], sems.at[step + 5]).start()
+
+    def sums_sent(unit, step):
+        planes, lines, totals = unit[1], unit[3], unit[5]
+        wait_bytes(planes.at[pl.ds(0, 31)], step)
+        wait_bytes(lines.at[pl.ds(0, 15)], step + 2)
+        wait_bytes(totals.at[pl.ds(0, 31)], step + 4)
+
+    def put_early(block, values):
+        early[0][4 * block : 4 * (block + 1)] = values.reshape(4, 32, 128)
+
+    def end_early():
+        wait_bytes(early[5], EARLY + 5)
+        targets = [proj_ref.at[1, :, pl.ds(128 * g, 128)] for g in range(5)]
+        targets += [out_ref.at[1], proj_ref.at[0, :, pl.ds(512, 128)], out_ref.at[0]]
+        for block, target in enumerate(targets):
+            values = early[5][4 * block : 4 * (block + 1)]
+            target[...] = values.reshape(128, 128).astype(F32)
+
+    def end_late():
+        wait_bytes(late[5], LATE + 5)
         for g in range(4):
-            values = all_buf[unit, 8 * g : 8 * (g + 1)].reshape(128, 128).astype(F32)
-            if unit == 1:
-                u = 1 - g // 2
-                if g % 2 == 0:
-                    proj_ref[u, :, 512:640] = values
-                else:
-                    out_ref[u] = values
-            else:
-                proj_ref[1 - unit // 2, :, 128 * g : 128 * (g + 1)] = values
+            values = late[5][8 * g : 8 * (g + 1)].reshape(128, 128)
+            proj_ref[0, :, 128 * g : 128 * (g + 1)] = values.astype(F32)
 
     def backward(u):
         each(4, lambda r: branch_back(u, r))
-        to_messages(cm, TO_OWNER, dprod_send, u, 1)
-        exchange(dprod_send, dprod_recv, u, D_PRODUCTS)
-        first = 0 if u == 1 else 16
-        sum_send[1, first : first + 8] = proj_part(u, 4)
-        sum_send[1, first + 8 : first + 16] = out_part(u)
+        send_messages(cm, TO_OWNER, dprod_send, dprod_recv, u, D_PRODUCTS, 1)
+        if u == 1:
+            put_early(5, out_part(1))
+            put_early(4, proj_part(1, 4))
+        else:
+            for g in range(4):
+                put_early(g, proj_part(1, g))
+            put_early(6, proj_part(0, 4))
+            put_early(7, out_part(0))
+            begin_sum(early, EARLY)
+        take_messages(dprod_recv, BY_CHANNEL, u, D_PRODUCTS, store_out, 1)
+        each(4, lambda h: multiply_back(u, h))
+        send_messages(own_out, BY_SOURCE, dedge_send, dedge_recv, u, D_EDGES, 2)
         if u == 0:
-            sum_begin(1)
-            sum_line(0)
-        arrive(dprod_recv, u, D_PRODUCTS)
-        from_messages(dprod_recv, BY_CHANNEL, u, store_out, 1)
-        each(4, lambda h: multiply_back(u, h))
-        to_messages(own_out, BY_SOURCE, dedge_send, u, 2)
-        exchange(dedge_send, dedge_recv, u, D_EDGES)
-        if u == 0:
-            sum_share(0)
-            sum_line(1)
-        arrive(dedge_recv, u, D_EDGES)
-        from_messages(dedge_recv, FROM_OWNER, u, store_cm(2), 2)
+            sum_line(early, EARLY)
+        take_messages(dedge_recv, FROM_OWNER, u, D_EDGES, store_cm(2), 2)
         each(4, lambda r: edges_back(u, r))
-        unit = 0 if u == 1 else 2
+        if u == 1:
+            each(4, lambda r: norm_back(1, r))
+
+    def finish():
         for g in range(4):
-            sum_send[unit, 8 * g : 8 * (g + 1)] = proj_part(u, g)
-        sum_begin(unit)
-        each(4, lambda r: norm_back(u, r))
+            values = proj_part(0, g)
+            late[0][8 * g : 8 * (g + 1)] = values.reshape(8, 16, 128)
+        begin_sum(late, LATE)
+        for r in range(4):
+            norm_back(0, r)
+            if r < 2:
+                send_grad(r)
+        share_sum(early, EARLY)
+        sum_line(late, LATE)
+        send_grad(2)
+        send_grad(3)
+        end_early()
+        share_sum(late, LATE)
+        end_late()
 
     loads = [
         pltpu.make_async_copy(source, target, sems.at[LOADS + k])
@@ -507,12 +539,7 @@
     forward(1)
     backward(1)
     backward(0)
-    sum_share(1)
-    sum_line(2)
-    sum_end(0)
-    sum_share(2)
-    sum_end(1)
-    sum_end(2)
+    finish()
     wait_bytes(grad_buf, GRAD_CAME)
     grad_ref[...] = grad_buf[...]
 
@@ -530,11 +557,9 @@
         (D_EDGES, dedge_send),
     ):
         for u in range(2):
-            wait_bytes(sent.at[u, pl.ds(0, 31)], 2 * (step + u))
-    for unit in range(3):
-        wait_bytes(plane_buf.at[unit, pl.ds(0, 31)], 2 * sum_step(unit, 0))
-        wait_bytes(z_buf.at[unit, pl.ds(0, 15)], 2 * sum_step(unit, 1))
-        wait_bytes(all_buf.at[unit, pl.ds(0, 31)], 2 * sum_step(unit, 2))
+            wait_bytes(sent.at[u, pl.ds(0, 31)], step + u)
+    sums_sent(early, EARLY)
+    sums_sent(late, LATE)
 
 
 def shards(
@@ -604,13 +629,19 @@
             half(2, 32, 16, 128),
             half(2, 32, 32, 128),
             half(2, 32, 32, 128),
-            half(3, 32, 16, 128),
-            half(3, 32, 16, 128),
-            half(3, 16, 128),
-            half(3, 16, 16, 128),
-            half(3, 16, 128),
-            half(3, 32, 16, 128),
-            pltpu.SemaphoreType.DMA((51,)),
+            half(32, 32, 128),
+            half(32, 32, 128),
+            half(32, 128),
+            half(16, 32, 128),
+            half(32, 128),
+            half(32, 32, 128),
+            half(32, 16, 128),
+            half(32, 16, 128),
+            half(16, 128),
+            half(16, 16, 128),
+            half(16, 128),
+            half(32, 16, 128),
+            pltpu.SemaphoreType.DMA((SEMAPHORES,)),
         ],
         compiler_params=pltpu.CompilerParams(
             collective_id=1, has_side_effects=True, vmem_limit_bytes=40 << 20

time: 117 us -> 114 us (0.974)
  Pallas kernels: 106 us -> 104 us
    pallas_call x1, Pallas kernels: 106 us -> 104 us  [shards(): pl.pallas_call(kernel, out_shape=(jax.ShapeDtypeStruct((4, 128, 128), BF1...]
where the time goes in v4:
time: 114 us; the launch traced here: 113 us
  Pallas kernels  104 us (91%)
  local copies, waits for them, and re-layouts  9.17 us (8%)
    pallas_call x1, Pallas kernels, shards(): pl.pallas_call(kernel, out_shape=(jax.ShapeDtypeStruct((4, 128, 128), BF1...  104 us
    unnamed x21, local copies, waits for them, and re-layouts  9.17 us

profile of v4, /device:TPU:1, one launch (start us, length us, event | category | flops | bytes accessed | tf_op | source)
XLA Modules:
  0.0 113.4 jit_solution(5921009008459492770)
XLA Ops:
  0.6 0.0 copy-start.4
  0.6 0.7 copy-done.4
  1.3 0.0 copy-start
  1.3 1.0 copy-done
  2.3 0.0 copy-start.1
  2.3 0.9 copy-done.1
  3.2 0.0 copy-start.2
  3.2 0.9 copy-done.2
  4.1 0.0 copy-start.3
  4.1 0.8 copy-done.3
  4.9 0.0 copy-start.5
  4.9 0.7 copy-done.5
  5.6 0.0 copy-start.6
  5.6 0.7 copy-done.6
  6.3 0.0 copy-start.7
  6.3 0.7 copy-done.7
  7.0 0.0 copy-start.8
  7.0 0.7 copy-done.8
  7.7 103.5 %shard_map.112 = (bf16[4,128,128]{2,1,0:T(8,128)(2,1)S(1)}, f32[2,128,640]{2,1,0:T(8,128)S(1)}, f32[2,128,128]{2,1,0:T(8,128)S(1)}) custom-call(bf16[4,128,128]{2,1,0:T(8,128)(2,1)S(1)} %bitcast.5, s32[4,128]{1,0:T(4,128)S(1)} %bitcast.7, bf16[4,128,128]{2,1,0:T(8,128)(2,1)S(1)} %bitcast.6, bf16[2,128,640]{2,1,0:T(8,128)(2,1)S(1)} %copy-done, ...), custom_call_target="tpu_custom_call" | custom-call | tf_op jit(solution)/shard_map/pallas_call | solution.py:583
  111.2 0.7 copy.15
  111.9 0.8 copy.16
  112.7 0.7 copy.17
Async XLA Ops:
  0.6 0.7 copy-start.4
  1.3 1.0 copy-start
  2.3 0.9 copy-start.1
  3.2 0.9 copy-start.2
  4.1 0.8 copy-start.3
  4.9 0.7 copy-start.5
  5.6 0.7 copy-start.6
  6.3 0.7 copy-start.7
  7.0 0.7 copy-start.8

commit v5 on v4

--- a/solution.py
+++ b/solution.py
@@ -644,7 +644,7 @@
             pltpu.SemaphoreType.DMA((SEMAPHORES,)),
         ],
         compiler_params=pltpu.CompilerParams(
-            collective_id=1, has_side_effects=True, vmem_limit_bytes=40 << 20
+            collective_id=1, has_side_effects=True, vmem_limit_bytes=63 << 20
         ),
     )(
         pair_repr[0],

time: 114 us -> 109 us (0.956)
  local copies, waits for them, and re-layouts: 9.17 us -> 4.23 us
    unnamed x21 -> x5, local copies, waits for them, and re-layouts: 9.17 us -> 4.23 us
where the time goes in v5:
time: 109 us
  Pallas kernels  104 us (95%)
  local copies, waits for them, and re-layouts  4.23 us (4%)
    pallas_call x1, Pallas kernels, shards(): pl.pallas_call(kernel, out_shape=(jax.ShapeDtypeStruct((4, 128, 128), BF1...  104 us
    unnamed x5, local copies, waits for them, and re-layouts  4.23 us

profile of v5, /device:TPU:1, one launch (start us, length us, event | category | flops | bytes accessed | tf_op | source)
XLA Modules:
  0.0 109.2 jit_solution(13087732362918734526)
XLA Ops:
  0.6 104.4 %shard_map.112 = (bf16[4,128,128]{2,1,0:T(8,128)(2,1)}, f32[2,128,640]{2,1,0:T(8,128)}, f32[2,128,128]{2,1,0:T(8,128)}) custom-call(bf16[4,128,128]{2,1,0:T(8,128)(2,1)} %bitcast.5, s32[4,128]{1,0:T(4,128)} %bitcast.7, bf16[4,128,128]{2,1,0:T(8,128)(2,1)} %bitcast.6, bf16[2,128,640]{2,1,0:T(8,128)(2,1)} %w_in.1, f32[2,640]{1,0:T(2,128)} %bias_in.1, ...), custom_call_target="tpu_custom_call" | custom-call | tf_op jit(solution)/shard_map/pallas_call | solution.py:583
  105.0 1.6 %copy.15 = bf16[1,4,128,128]{3,2,1,0:T(8,128)(2,1)} copy(bf16[1,4,128,128]{3,2,1,0:T(8,128)(2,1)} %bitcast.4) | data formatting | bytes 262144
  106.6 0.0 copy-start
  106.6 2.0 %copy.16 = f32[2,128,640]{2,1,0:T(8,128)} copy(f32[2,128,640]{2,1,0:T(8,128)} %get-tuple-element.13) | data formatting | bytes 1310720
  108.6 0.0 copy-done
  108.6 0.7 copy.17
Async XLA Ops:
  106.6 2.0 %copy-start = (f32[2,128,128]{2,1,0:T(8,128)S(1)}, f32[2,128,128]{2,1,0:T(8,128)}, u32[]{:S(2)}) copy-start(f32[2,128,128]{2,1,0:T(8,128)} %get-tuple-element.14) | copy-start | bytes 393220

commit v6 on v5

--- a/solution.py
+++ b/solution.py
@@ -462,13 +462,13 @@
         targets += [out_ref.at[1], proj_ref.at[0, :, pl.ds(512, 128)], out_ref.at[0]]
         for block, target in enumerate(targets):
             values = early[5][4 * block : 4 * (block + 1)]
-            target[...] = values.reshape(128, 128).astype(F32)
+            target[...] = values.reshape(128, 128)
 
     def end_late():
         wait_bytes(late[5], LATE + 5)
         for g in range(4):
             values = late[5][8 * g : 8 * (g + 1)].reshape(128, 128)
-            proj_ref[0, :, 128 * g : 128 * (g + 1)] = values.astype(F32)
+            proj_ref[0, :, 128 * g : 128 * (g + 1)] = values
 
     def backward(u):
         each(4, lambda r: branch_back(u, r))
@@ -501,8 +501,8 @@
             norm_back(0, r)
             if r < 2:
                 send_grad(r)
+        sum_line(late, LATE)
         share_sum(early, EARLY)
-        sum_line(late, LATE)
         send_grad(2)
         send_grad(3)
         end_early()
@@ -562,6 +562,12 @@
     sums_sent(late, LATE)
 
 
+def widen_kernel(grad_in, proj_in, out_in, grad_ref, proj_ref, out_ref):
+    grad_ref[...] = grad_in[...]
+    proj_ref[...] = proj_in[...].astype(F32)
+    out_ref[...] = out_in[...].astype(F32)
+
+
 def shards(
     pair_repr,
     pair_mask,
@@ -584,8 +590,8 @@
         kernel,
         out_shape=(
             jax.ShapeDtypeStruct((4, 128, 128), BF16),
-            jax.ShapeDtypeStruct((2, 128, 640), F32),
-            jax.ShapeDtypeStruct((2, 128, 128), F32),
+            jax.ShapeDtypeStruct((2, 128, 640), BF16),
+            jax.ShapeDtypeStruct((2, 128, 128), BF16),
         ),
         in_specs=[pl.BlockSpec(memory_space=pl.ANY)] * 9,
         out_specs=(vmem, vmem, vmem),
@@ -657,6 +663,17 @@
         out_weight,
         out_bias,
     )
+    pair_grad, proj_grad, out_grad = pl.pallas_call(
+        widen_kernel,
+        out_shape=(
+            jax.ShapeDtypeStruct((4, 128, 128), BF16),
+            jax.ShapeDtypeStruct((2, 128, 640), F32),
+            jax.ShapeDtypeStruct((2, 128, 128), F32),
+        ),
+        in_specs=[vmem] * 3,
+        out_specs=(vmem,) * 3,
+        compiler_params=pltpu.CompilerParams(vmem_limit_bytes=63 << 20),
+    )(pair_grad, proj_grad, out_grad)
     return pair_grad[None], proj_grad, out_grad
 
 

time: 109 us -> 107 us (0.982)
  local copies, waits for them, and re-layouts: 4.23 us -> 0 us
  Pallas kernels: 104 us -> 106 us
    unnamed x5 -> x0, local copies, waits for them, and re-layouts: 4.23 us -> none
    pallas_call x0 -> x1, Pallas kernels: none -> 1.97 us  [shards(): pl.pallas_call(widen_kernel, out_shape=(jax.ShapeDtypeStruct((4, 128, 128...]
where the time goes in v6:
time: 107 us; the launch traced here: 106 us
  Pallas kernels  106 us (99%)
    pallas_call x1, Pallas kernels, shards(): pl.pallas_call(kernel, out_shape=(jax.ShapeDtypeStruct((4, 128, 128), BF1...  104 us

profile of v6, /device:TPU:1, one launch (start us, length us, event | category | flops | bytes accessed | tf_op | source)
XLA Modules:
  0.0 106.3 jit_solution(15047505077025619089)
XLA Ops:
  0.6 103.7 %shard_map.112 = (bf16[4,128,128]{2,1,0:T(8,128)(2,1)}, bf16[2,128,640]{2,1,0:T(8,128)(2,1)}, bf16[2,128,128]{2,1,0:T(8,128)(2,1)}) custom-call(bf16[4,128,128]{2,1,0:T(8,128)(2,1)} %bitcast.4, s32[4,128]{1,0:T(4,128)} %bitcast.6, bf16[4,128,128]{2,1,0:T(8,128)(2,1)} %bitcast.5, bf16[2,128,640]{2,1,0:T(8,128)(2,1)} %w_in.1, f32[2,640]{1,0:T(2,128)} %bias_in.1, ...), custom_call_target="tpu_custom_call" | custom-call | tf_op jit(solution)/shard_map/pallas_call | solution.py:589
  104.4 2.0 %shard_map.113 = (bf16[4,128,128]{2,1,0:T(8,128)(2,1)}, f32[2,128,640]{2,1,0:T(8,128)}, f32[2,128,128]{2,1,0:T(8,128)}) custom-call(bf16[4,128,128]{2,1,0:T(8,128)(2,1)} %get-tuple-element.9.grad_in, bf16[2,128,640]{2,1,0:T(8,128)(2,1)} %get-tuple-element.10.proj_in, bf16[2,128,128]{2,1,0:T(8,128)(2,1)} %get-tuple-element.11.out_in), custom_call_target="tpu_custom_call" | custom-call | tf_op jit(solution)/shard_map/pallas_call | solution.py:666
